TPU v7x, 256 devices: a whole 4x4x8 slice. The times are simulated.
256 devices in a mesh: gx: 16 (over z, core), gy: 16 (over y, x).
Axes of the slice: x: 4, y: 4, z: 8, core: 2. Of those that a mesh axis runs over, the one named last changes fastest.
Arguments:
- forward_state: float32 [9, 4, 256, 2048], P(None, None, 'gx', 'gy'), may hold values from -22 to 22
- adjoint_state: float32 [9, 4, 256, 2048], P(None, None, 'gx', 'gy'), may hold values from -22 to 22
- phase_labels: int32 [4, 256, 2048], P(None, 'gx', 'gy'), may hold values from 0 to 3
- phase_table: float32 [3, 4], replicated, may hold values from 0.5 to 1.5
- source_cells: int32 [512], replicated, may hold values from 0 to 2097151
- wavelet: float32 [4, 512], replicated, may hold values from -24 to 24
- receiver_cells: int32 [1024], replicated, may hold values from 0 to 2097151
- residual_traces: float32 [4, 1024], replicated, may hold values from -24 to 24
Outputs:
- adjoint_final: float32 [9, 4, 256, 2048], P(None, None, 'gx', 'gy')
- grad_lambda: float32 [4, 256, 2048], P(None, 'gx', 'gy')
- grad_mu: float32 [4, 256, 2048], P(None, 'gx', 'gy')
All inputs are finite; a program needn't handle non-finite values.
Results may differ from a plain program's by a relative error of at most 0.00002.
Values sent between devices are 32-bit elements; how exact they have to be, the bound alone decides.
A program may use at most 128 MiB of HBM per device.

v0:
```python
import jax
import jax.numpy as jnp
from jax import lax
from jax.sharding import PartitionSpec as P

coeffs = (1225.0 / 1024.0, -245.0 / 3072.0, 49.0 / 5120.0, -5.0 / 7168.0)
step_dt = 0.1


def padded_2(block, sides, width):
    for axis, dim in sides:
        count = lax.axis_size(axis)
        forward = [(i, i + 1) for i in range(count - 1)]
        backward = [(target, source) for source, target in forward]
        low = lax.ppermute(
            lax.slice_in_dim(block, block.shape[dim] - width, None, axis=dim), axis, forward
        )
        high = lax.ppermute(lax.slice_in_dim(block, 0, width, axis=dim), axis, backward)
        block = jnp.concatenate([low, block, high], axis=dim)
    return block


def shift_diff(field, axis, plus):
    length = field.shape[axis] - 8
    total = jnp.zeros(field.shape[:axis] + (length,) + field.shape[axis + 1 :], jnp.float32)
    for k in range(1, 5):
        first = 4 + k if plus else 3 + k
        second = 5 - k if plus else 4 - k
        total = total + coeffs[k - 1] * (
            lax.slice_in_dim(field, first, first + length, axis=axis)
            - lax.slice_in_dim(field, second, second + length, axis=axis)
        )
    return total


def deriv(field, axis, plus):
    if axis == 0:
        padded = jnp.pad(field, ((4, 4), (0, 0), (0, 0)))
        return shift_diff(padded, 0, plus)[:, 4:-4, 4:-4]
    if axis == 1:
        return shift_diff(field, 1, plus)[:, :, 4:-4]
    return shift_diff(field, 2, plus)[:, 4:-4, :]


def divergence(stress_list):
    sxx, syy, szz, sxy, sxz, syz = stress_list
    return [
        deriv(sxx, 1, True) + deriv(sxy, 2, False) + deriv(sxz, 0, False),
        deriv(sxy, 1, False) + deriv(syy, 2, True) + deriv(syz, 0, False),
        deriv(sxz, 1, False) + deriv(syz, 2, False) + deriv(szz, 0, True),
    ]


def strains(vel_list):
    vx, vy, vz = vel_list
    return [
        deriv(vx, 1, False),
        deriv(vy, 2, False),
        deriv(vz, 0, False),
        deriv(vx, 2, True) + deriv(vy, 1, True),
        deriv(vx, 0, True) + deriv(vz, 1, True),
        deriv(vy, 0, True) + deriv(vz, 2, True),
    ]


def stress_inc(strain_list, lam, shear):
    trace = strain_list[0] + strain_list[1] + strain_list[2]
    normal = [lam * trace + 2.0 * shear * strain_list[i] for i in range(3)]
    return normal + [shear * strain_list[i] for i in range(3, 6)]


def materials(labels, table):
    lam = jnp.zeros(labels.shape, jnp.float32)
    shear = jnp.zeros(labels.shape, jnp.float32)
    dense = jnp.zeros(labels.shape, jnp.float32)
    for phase in range(table.shape[1]):
        match = labels == phase
        lam = lam + jnp.where(match, table[0, phase], 0.0)
        shear = shear + jnp.where(match, table[1, phase], 0.0)
        dense = dense + jnp.where(match, table[2, phase], 0.0)
    return (lam, shear, 1.0 / dense)


def inject(field, cells, values, cells_x, cells_y):
    total_x = cells_x * lax.axis_size("gx")
    total_y = cells_y * lax.axis_size("gy")
    layer = cells // (total_x * total_y)
    local_x = cells // total_y % total_x - lax.axis_index("gx") * cells_x
    local_y = cells % total_y - lax.axis_index("gy") * cells_y
    valid = (
        (local_x >= 0) & (local_x < field.shape[1]) & (local_y >= 0) & (local_y < field.shape[2])
    )
    safe_x = jnp.where(valid, local_x, field.shape[1])
    safe_y = jnp.where(valid, local_y, field.shape[2])
    return field.at[layer, safe_x, safe_y].add(jnp.where(valid, values, 0.0), mode="drop")


def stress_halo(stack):
    return padded_2(stack, (("gx", 2), ("gy", 3)), 4)


def velocity_halo(stack):
    return padded_2(stack, (("gx", 2), ("gy", 3)), 4)


def halo_divergence(stress_list):
    wide = stress_halo(jnp.stack(stress_list))
    return divergence([wide[i] for i in range(6)])


def rim_strains(vel_list):
    wide = velocity_halo(jnp.stack(vel_list))
    return strains([wide[i] for i in range(3)])


def accumulate(grad_lambda, grad_mu, fwd, adj_strain):
    trace_f = fwd[0] + fwd[1] + fwd[2]
    trace_a = adj_strain[0] + adj_strain[1] + adj_strain[2]
    grad_lambda = grad_lambda + step_dt * trace_f * trace_a
    pair = 2.0 * (fwd[0] * adj_strain[0] + fwd[1] * adj_strain[1] + fwd[2] * adj_strain[2])
    pair = pair + fwd[3] * adj_strain[3] + fwd[4] * adj_strain[4] + fwd[5] * adj_strain[5]
    return (grad_lambda, grad_mu + step_dt * pair)


def shards(
    forward_state,
    adjoint_state,
    phase_labels,
    phase_table,
    source_cells,
    wavelet,
    receiver_cells,
    residual_traces,
):
    cells_x = phase_labels.shape[1]
    cells_y = phase_labels.shape[2]
    steps_count = wavelet.shape[0]
    lam, shear, buoy = materials(phase_labels, phase_table)
    vel = [forward_state[i] for i in range(3)]
    stress = [forward_state[i] for i in range(3, 9)]
    adj_vel = [adjoint_state[i] for i in range(3)]
    adj_stress = [adjoint_state[i] for i in range(3, 9)]
    grad_lambda = jnp.zeros(phase_labels.shape, jnp.float32)
    grad_mu = jnp.zeros(phase_labels.shape, jnp.float32)
    saved = []
    for step in range(steps_count):
        div = halo_divergence(stress)
        vel = [vel[i] + step_dt * buoy * div[i] for i in range(3)]
        vel[2] = inject(vel[2], source_cells, step_dt * wavelet[step], cells_x, cells_y)
        strain_now = rim_strains(vel)
        inc = stress_inc(strain_now, lam, shear)
        stress = [stress[i] + step_dt * inc[i] for i in range(6)]
        saved.append(strain_now)
    for step in range(steps_count):
        adj_strain = rim_strains(adj_vel)
        inc = stress_inc(adj_strain, lam, shear)
        adj_stress = [adj_stress[i] - step_dt * inc[i] for i in range(6)]
        div = halo_divergence(adj_stress)
        adj_vel = [adj_vel[i] - step_dt * buoy * div[i] for i in range(3)]
        adj_vel[2] = inject(
            adj_vel[2], receiver_cells, step_dt * residual_traces[step], cells_x, cells_y
        )
        grad_lambda, grad_mu = accumulate(
            grad_lambda, grad_mu, saved[steps_count - 1 - step], adj_strain
        )
    return (jnp.stack(adj_vel + adj_stress), grad_lambda, grad_mu)


def solution(mesh):
    placed = (
        P(None, None, "gx", "gy"),
        P(None, None, "gx", "gy"),
        P(None, "gx", "gy"),
        P(),
        P(),
        P(),
        P(),
        P(),
    )
    return jax.shard_map(
        shards,
        mesh=mesh,
        in_specs=placed,
        out_specs=(P(None, None, "gx", "gy"), P(None, "gx", "gy"), P(None, "gx", "gy")),
        check_vma=False,
    )
```

profile of v0, /device:TPU:103, one launch (start us, length us, event | category | flops | bytes accessed | tf_op | source)
XLA Modules:
  0.0 647.5 jit_solution(5710287187535147140)
XLA Ops:
  1.6 5.3 collective-permute-start
  10.0 4.9 collective-permute-start.32
  27.1 5.2 collective-permute-start.2
  42.1 31.0 %scatter_fusion = f32[4,16,128]{2,1,0:T(8,128)S(1)} fusion(f32[4,16,128]{2,1,0:T(8,128)S(1)} %fusion.495, s32[512]{0:T(512)S(1)} %bitcast.392, f32[512]{0:T(512)S(1)} %get-tuple-element.1346), kind=kCustom, calls=%fused_computation | custom fusion | flops 512 | bytes 12288 | tf_op jit(solution)/shard_map/scatter-add | solution.py:95
  75.8 4.6 collective-permute-start.36
  82.6 4.2 collective-permute-done.37
  86.9 5.0 collective-permute-start.38
  94.0 5.9 collective-permute-done.39
  101.0 5.3 constant_dynamic-update-slice_fusion.38
  112.2 4.6 collective-permute-done.41
  135.6 31.0 %scatter_fusion.1 = f32[4,16,128]{2,1,0:T(8,128)S(1)} fusion(f32[4,16,128]{2,1,0:T(8,128)S(1)} %fusion.357, s32[512]{0:T(512)S(1)} %bitcast.393, f32[512]{0:T(512)S(1)} %get-tuple-element.1345), kind=kCustom, calls=%fused_computation.1 | custom fusion | flops 512 | bytes 12288 | tf_op jit(solution)/shard_map/scatter-add | solution.py:95
  179.5 4.4 collective-permute-done.45
  209.7 4.7 collective-permute-done.49
  222.5 4.4 collective-permute-done.51
  233.8 31.0 %scatter_fusion.2 = f32[4,16,128]{2,1,0:T(8,128)S(1)} fusion(f32[4,16,128]{2,1,0:T(8,128)S(1)} %fusion.219, s32[512]{0:T(512)S(1)} %bitcast.394, f32[512]{0:T(512)S(1)} %copy-done.226), kind=kCustom, calls=%fused_computation.2 | custom fusion | flops 512 | bytes 12288 | tf_op jit(solution)/shard_map/scatter-add | solution.py:95
  278.3 4.1 collective-permute-done.53
  332.1 6.1 scatter_fusion.4
  351.0 4.4 collective-permute-done.9
  383.8 4.9 collective-permute-start.12
  408.1 4.2 collective-permute-done.15
  420.7 31.0 %scatter_fusion.3 = f32[4,16,128]{2,1,0:T(8,128)S(1)} fusion(f32[4,16,128]{2,1,0:T(8,128)S(1)} %fusion.79, s32[512]{0:T(512)S(1)} %bitcast.395, f32[512]{0:T(512)S(1)} %copy-done.225), kind=kCustom, calls=%fused_computation.3 | custom fusion | flops 512 | bytes 12288 | tf_op jit(solution)/shard_map/scatter-add | solution.py:95
  451.8 4.2 fusion.104
  460.6 4.2 collective-permute-start.60
  472.3 6.1 scatter_fusion.5
  485.2 4.9 collective-permute-start.16
  522.5 5.9 collective-permute-start.20
  543.1 5.5 collective-permute-done.23
  556.2 6.1 scatter_fusion.6
  562.5 4.2 fusion.732
  575.2 4.4 collective-permute-done.25
  610.6 4.7 collective-permute-done.29
  631.7 6.1 scatter_fusion.7
  (875 shorter events, 379.0 us)
Async XLA Ops:
  1.6 18.6 %collective-permute-start = (f32[3,4,4,128]{3,2,1,0:T(4,128)S(1)}, f32[3,4,4,128]{3,2,1,0:T(4,128)S(1)}, u32[]{:S(2)}, u32[]{:S(2)}) collective-permute-start(f32[3,4,4,128]{3,2,1,0:T(4,128)S(1)} %get-tuple-element.201), channel_id=1, source_target_pairs={{0,16},{16,32},{32,48},{48,64},{64,80},{80,96},{96,112},{112,128},... | collective-permute-start | bytes 73736 | tf_op jit(solution)/shard_map/ppermute | solution.py:15
  7.0 13.2 %collective-permute-start.1 = (f32[3,4,4,128]{3,2,1,0:T(4,128)S(1)}, f32[3,4,4,128]{3,2,1,0:T(4,128)S(1)}, u32[]{:S(2)}, u32[]{:S(2)}) collective-permute-start(f32[3,4,4,128]{3,2,1,0:T(4,128)S(1)} %get-tuple-element.202), channel_id=1, source_target_pairs={{16,0},{32,16},{48,32},{64,48},{80,64},{96,80},{112,96},{128,112},... | collective-permute-start | bytes 73736 | tf_op jit(solution)/shard_map/ppermute | solution.py:18
  10.0 10.2 %collective-permute-start.32 = (f32[6,4,4,128]{3,2,1,0:T(4,128)S(1)}, f32[6,4,4,128]{3,2,1,0:T(4,128)S(1)}, u32[]{:S(2)}, u32[]{:S(2)}) collective-permute-start(f32[6,4,4,128]{3,2,1,0:T(4,128)S(1)} %get-tuple-element.208), channel_id=1, source_target_pairs={{0,16},{16,32},{32,48},{48,64},{64,80},{80,96},{96,112},{112,128},... | collective-permute-start | bytes 147464 | tf_op jit(solution)/shard_map/ppermute | solution.py:15
  21.7 12.6 %collective-permute-start.34 = (f32[6,4,24,4]{3,2,1,0:T(8,128)S(1)}, f32[6,4,24,4]{3,2,1,0:T(8,128)S(1)}, u32[]{:S(2)}, u32[]{:S(2)}) collective-permute-start(f32[6,4,24,4]{3,2,1,0:T(8,128)S(1)} %get-tuple-element.206), channel_id=1, source_target_pairs={{0,1},{1,2},{2,3},{3,4},{4,5},{5,6},{6,7},{7,8},{8,9},{9,10},{10,1... | collective-permute-start | bytes 27656 | tf_op jit(solution)/shard_map/ppermute | solution.py:15
  24.8 10.0 %collective-permute-start.35 = (f32[6,4,24,4]{3,2,1,0:T(8,128)S(1)}, f32[6,4,24,4]{3,2,1,0:T(8,128)S(1)}, u32[]{:S(2)}, u32[]{:S(2)}) collective-permute-start(f32[6,4,24,4]{3,2,1,0:T(8,128)S(1)} %get-tuple-element.207), channel_id=1, source_target_pairs={{1,0},{2,1},{3,2},{4,3},{5,4},{6,5},{7,6},{8,7},{9,8},{10,9},{11,1... | collective-permute-start | bytes 27656 | tf_op jit(solution)/shard_map/ppermute | solution.py:18
  27.1 55.3 %collective-permute-start.2 = (f32[3,4,24,4]{3,2,1,0:T(8,128)S(1)}, f32[3,4,24,4]{3,2,1,0:T(8,128)S(1)}, u32[]{:S(2)}, u32[]{:S(2)}) collective-permute-start(f32[3,4,24,4]{3,2,1,0:T(8,128)S(1)} %get-tuple-element.236), channel_id=1, source_target_pairs={{0,1},{1,2},{2,3},{3,4},{4,5},{5,6},{6,7},{7,8},{8,9},{9,10},{10,1... | collective-permute-start | bytes 13832 | tf_op jit(solution)/shard_map/ppermute | solution.py:15
  32.3 50.0 %collective-permute-start.3 = (f32[3,4,24,4]{3,2,1,0:T(8,128)S(1)}, f32[3,4,24,4]{3,2,1,0:T(8,128)S(1)}, u32[]{:S(2)}, u32[]{:S(2)}) collective-permute-start(f32[3,4,24,4]{3,2,1,0:T(8,128)S(1)} %get-tuple-element.237), channel_id=1, source_target_pairs={{1,0},{2,1},{3,2},{4,3},{5,4},{6,5},{7,6},{8,7},{9,8},{10,9},{11,1... | collective-permute-start | bytes 13832 | tf_op jit(solution)/shard_map/ppermute | solution.py:18
  91.9 8.0 %collective-permute-start.39 = (f32[3,4,24,4]{3,2,1,0:T(8,128)S(1)}, f32[3,4,24,4]{3,2,1,0:T(8,128)S(1)}, u32[]{:S(2)}, u32[]{:S(2)}) collective-permute-start(f32[3,4,24,4]{3,2,1,0:T(8,128)S(1)} %get-tuple-element.239), channel_id=1, source_target_pairs={{1,0},{2,1},{3,2},{4,3},{5,4},{6,5},{7,6},{8,7},{9,8},{10,9},{11,1... | collective-permute-start | bytes 13832 | tf_op jit(solution)/shard_map/ppermute | solution.py:18
  118.9 9.7 %collective-permute-start.43 = (f32[6,4,24,4]{3,2,1,0:T(8,128)S(1)}, f32[6,4,24,4]{3,2,1,0:T(8,128)S(1)}, u32[]{:S(2)}, u32[]{:S(2)}) collective-permute-start(f32[6,4,24,4]{3,2,1,0:T(8,128)S(1)} %get-tuple-element.185), channel_id=1, source_target_pairs={{1,0},{2,1},{3,2},{4,3},{5,4},{6,5},{7,6},{8,7},{9,8},{10,9},{11,1... | collective-permute-start | bytes 27656 | tf_op jit(solution)/shard_map/ppermute | solution.py:18
  184.1 8.3 %collective-permute-start.46 = (f32[3,4,24,4]{3,2,1,0:T(8,128)S(1)}, f32[3,4,24,4]{3,2,1,0:T(8,128)S(1)}, u32[]{:S(2)}, u32[]{:S(2)}) collective-permute-start(f32[3,4,24,4]{3,2,1,0:T(8,128)S(1)} %get-tuple-element.230), channel_id=1, source_target_pairs={{0,1},{1,2},{2,3},{3,4},{4,5},{5,6},{6,7},{7,8},{8,9},{9,10},{10,1... | collective-permute-start | bytes 13832 | tf_op jit(solution)/shard_map/ppermute | solution.py:15
  186.0 8.0 %collective-permute-start.47 = (f32[3,4,24,4]{3,2,1,0:T(8,128)S(1)}, f32[3,4,24,4]{3,2,1,0:T(8,128)S(1)}, u32[]{:S(2)}, u32[]{:S(2)}) collective-permute-start(f32[3,4,24,4]{3,2,1,0:T(8,128)S(1)} %get-tuple-element.231), channel_id=1, source_target_pairs={{1,0},{2,1},{3,2},{4,3},{5,4},{6,5},{7,6},{8,7},{9,8},{10,9},{11,1... | collective-permute-start | bytes 13832 | tf_op jit(solution)/shard_map/ppermute | solution.py:18
  216.5 10.3 %collective-permute-start.51 = (f32[6,4,24,4]{3,2,1,0:T(8,128)S(1)}, f32[6,4,24,4]{3,2,1,0:T(8,128)S(1)}, u32[]{:S(2)}, u32[]{:S(2)}) collective-permute-start(f32[6,4,24,4]{3,2,1,0:T(8,128)S(1)} %get-tuple-element.180), channel_id=1, source_target_pairs={{1,0},{2,1},{3,2},{4,3},{5,4},{6,5},{7,6},{8,7},{9,8},{10,9},{11,1... | collective-permute-start | bytes 27656 | tf_op jit(solution)/shard_map/ppermute | solution.py:18
  284.5 8.0 %collective-permute-start.55 = (f32[3,4,24,4]{3,2,1,0:T(8,128)S(1)}, f32[3,4,24,4]{3,2,1,0:T(8,128)S(1)}, u32[]{:S(2)}, u32[]{:S(2)}) collective-permute-start(f32[3,4,24,4]{3,2,1,0:T(8,128)S(1)} %get-tuple-element.229), channel_id=1, source_target_pairs={{1,0},{2,1},{3,2},{4,3},{5,4},{6,5},{7,6},{8,7},{9,8},{10,9},{11,1... | collective-permute-start | bytes 13832 | tf_op jit(solution)/shard_map/ppermute | solution.py:18
  314.8 9.7 %collective-permute-start.7 = (f32[6,4,24,4]{3,2,1,0:T(8,128)S(1)}, f32[6,4,24,4]{3,2,1,0:T(8,128)S(1)}, u32[]{:S(2)}, u32[]{:S(2)}) collective-permute-start(f32[6,4,24,4]{3,2,1,0:T(8,128)S(1)} %get-tuple-element.197), channel_id=1, source_target_pairs={{1,0},{2,1},{3,2},{4,3},{5,4},{6,5},{7,6},{8,7},{9,8},{10,9},{11,1... | collective-permute-start | bytes 27656 | tf_op jit(solution)/shard_map/ppermute | solution.py:18
  375.7 14.9 %collective-permute-start.56 = (f32[6,4,4,128]{3,2,1,0:T(4,128)S(1)}, f32[6,4,4,128]{3,2,1,0:T(4,128)S(1)}, u32[]{:S(2)}, u32[]{:S(2)}) collective-permute-start(f32[6,4,4,128]{3,2,1,0:T(4,128)S(1)} %get-tuple-element.212), channel_id=1, source_target_pairs={{0,16},{16,32},{32,48},{48,64},{64,80},{80,96},{96,112},{112,128},... | collective-permute-start | bytes 147464 | tf_op jit(solution)/shard_map/ppermute | solution.py:15
  378.8 11.8 %collective-permute-start.57 = (f32[6,4,4,128]{3,2,1,0:T(4,128)S(1)}, f32[6,4,4,128]{3,2,1,0:T(4,128)S(1)}, u32[]{:S(2)}, u32[]{:S(2)}) collective-permute-start(f32[6,4,4,128]{3,2,1,0:T(4,128)S(1)} %get-tuple-element.213), channel_id=1, source_target_pairs={{16,0},{32,16},{48,32},{64,48},{80,64},{96,80},{112,96},{128,112},... | collective-permute-start | bytes 147464 | tf_op jit(solution)/shard_map/ppermute | solution.py:18
  383.8 12.3 %collective-permute-start.12 = (f32[6,4,4,128]{3,2,1,0:T(4,128)S(1)}, f32[6,4,4,128]{3,2,1,0:T(4,128)S(1)}, u32[]{:S(2)}, u32[]{:S(2)}) collective-permute-start(f32[6,4,4,128]{3,2,1,0:T(4,128)S(1)} %get-tuple-element.220), channel_id=1, source_target_pairs={{0,16},{16,32},{32,48},{48,64},{64,80},{80,96},{96,112},{112,128},... | collective-permute-start | bytes 147464 | tf_op jit(solution)/shard_map/ppermute | solution.py:15
  390.8 11.5 %collective-permute-start.58 = (f32[6,4,24,4]{3,2,1,0:T(8,128)S(1)}, f32[6,4,24,4]{3,2,1,0:T(8,128)S(1)}, u32[]{:S(2)}, u32[]{:S(2)}) collective-permute-start(f32[6,4,24,4]{3,2,1,0:T(8,128)S(1)} %get-tuple-element.174), channel_id=1, source_target_pairs={{0,1},{1,2},{2,3},{3,4},{4,5},{5,6},{6,7},{7,8},{8,9},{9,10},{10,1... | collective-permute-start | bytes 27656 | tf_op jit(solution)/shard_map/ppermute | solution.py:15
  392.7 11.3 %collective-permute-start.59 = (f32[6,4,24,4]{3,2,1,0:T(8,128)S(1)}, f32[6,4,24,4]{3,2,1,0:T(8,128)S(1)}, u32[]{:S(2)}, u32[]{:S(2)}) collective-permute-start(f32[6,4,24,4]{3,2,1,0:T(8,128)S(1)} %get-tuple-element.175), channel_id=1, source_target_pairs={{1,0},{2,1},{3,2},{4,3},{5,4},{6,5},{7,6},{8,7},{9,8},{10,9},{11,1... | collective-permute-start | bytes 27656 | tf_op jit(solution)/shard_map/ppermute | solution.py:18
  396.3 11.8 %collective-permute-start.14 = (f32[6,4,24,4]{3,2,1,0:T(8,128)S(1)}, f32[6,4,24,4]{3,2,1,0:T(8,128)S(1)}, u32[]{:S(2)}, u32[]{:S(2)}) collective-permute-start(f32[6,4,24,4]{3,2,1,0:T(8,128)S(1)} %get-tuple-element.191), channel_id=1, source_target_pairs={{0,1},{1,2},{2,3},{3,4},{4,5},{5,6},{6,7},{7,8},{8,9},{9,10},{10,1... | collective-permute-start | bytes 27656 | tf_op jit(solution)/shard_map/ppermute | solution.py:15
  400.3 11.9 %collective-permute-start.15 = (f32[6,4,24,4]{3,2,1,0:T(8,128)S(1)}, f32[6,4,24,4]{3,2,1,0:T(8,128)S(1)}, u32[]{:S(2)}, u32[]{:S(2)}) collective-permute-start(f32[6,4,24,4]{3,2,1,0:T(8,128)S(1)} %get-tuple-element.192), channel_id=1, source_target_pairs={{1,0},{2,1},{3,2},{4,3},{5,4},{6,5},{7,6},{8,7},{9,8},{10,9},{11,1... | collective-permute-start | bytes 27656 | tf_op jit(solution)/shard_map/ppermute | solution.py:18
  460.6 31.4 %collective-permute-start.60 = (f32[3,4,4,128]{3,2,1,0:T(4,128)}, f32[3,4,4,128]{3,2,1,0:T(4,128)S(1)}, u32[]{:S(2)}, u32[]{:S(2)}) collective-permute-start(f32[3,4,4,128]{3,2,1,0:T(4,128)} %get-tuple-element.484), channel_id=1, source_target_pairs={{0,16},{16,32},{32,48},{48,64},{64,80},{80,96},{96,112},{112,128},... | collective-permute-start | bytes 73736 | tf_op jit(solution)/shard_map/ppermute | solution.py:15
  464.8 27.2 %collective-permute-start.61 = (f32[3,4,4,128]{3,2,1,0:T(4,128)}, f32[3,4,4,128]{3,2,1,0:T(4,128)}, u32[]{:S(2)}, u32[]{:S(2)}) collective-permute-start(f32[3,4,4,128]{3,2,1,0:T(4,128)} %get-tuple-element.485), channel_id=1, source_target_pairs={{16,0},{32,16},{48,32},{64,48},{80,64},{96,80},{112,96},{128,112},... | collective-permute-start | bytes 73736 | tf_op jit(solution)/shard_map/ppermute | solution.py:18
  485.2 13.0 %collective-permute-start.16 = (f32[3,4,4,128]{3,2,1,0:T(4,128)S(1)}, f32[3,4,4,128]{3,2,1,0:T(4,128)S(1)}, u32[]{:S(2)}, u32[]{:S(2)}) collective-permute-start(f32[3,4,4,128]{3,2,1,0:T(4,128)S(1)} %get-tuple-element.952), channel_id=1, source_target_pairs={{0,16},{16,32},{32,48},{48,64},{64,80},{80,96},{96,112},{112,128},... | collective-permute-start | bytes 73736 | tf_op jit(solution)/shard_map/ppermute | solution.py:15
  490.1 8.1 %collective-permute-start.17 = (f32[3,4,4,128]{3,2,1,0:T(4,128)S(1)}, f32[3,4,4,128]{3,2,1,0:T(4,128)S(1)}, u32[]{:S(2)}, u32[]{:S(2)}) collective-permute-start(f32[3,4,4,128]{3,2,1,0:T(4,128)S(1)} %get-tuple-element.953), channel_id=1, source_target_pairs={{16,0},{32,16},{48,32},{64,48},{80,64},{96,80},{112,96},{128,112},... | collective-permute-start | bytes 73736 | tf_op jit(solution)/shard_map/ppermute | solution.py:18
  492.9 11.7 %collective-permute-start.62 = (f32[3,4,24,4]{3,2,1,0:T(8,128)S(1)}, f32[3,4,24,4]{3,2,1,0:T(8,128)S(1)}, u32[]{:S(2)}, u32[]{:S(2)}) collective-permute-start(f32[3,4,24,4]{3,2,1,0:T(8,128)S(1)} %get-tuple-element.226), channel_id=1, source_target_pairs={{0,1},{1,2},{2,3},{3,4},{4,5},{5,6},{6,7},{7,8},{8,9},{9,10},{10,1... | collective-permute-start | bytes 13832 | tf_op jit(solution)/shard_map/ppermute | solution.py:15
  494.8 9.8 %collective-permute-start.63 = (f32[3,4,24,4]{3,2,1,0:T(8,128)S(1)}, f32[3,4,24,4]{3,2,1,0:T(8,128)S(1)}, u32[]{:S(2)}, u32[]{:S(2)}) collective-permute-start(f32[3,4,24,4]{3,2,1,0:T(8,128)S(1)} %get-tuple-element.227), channel_id=1, source_target_pairs={{1,0},{2,1},{3,2},{4,3},{5,4},{6,5},{7,6},{8,7},{9,8},{10,9},{11,1... | collective-permute-start | bytes 13832 | tf_op jit(solution)/shard_map/ppermute | solution.py:18
  498.4 10.8 %collective-permute-start.18 = (f32[3,4,24,4]{3,2,1,0:T(8,128)S(1)}, f32[3,4,24,4]{3,2,1,0:T(8,128)S(1)}, u32[]{:S(2)}, u32[]{:S(2)}) collective-permute-start(f32[3,4,24,4]{3,2,1,0:T(8,128)S(1)} %get-tuple-element.232), channel_id=1, source_target_pairs={{0,1},{1,2},{2,3},{3,4},{4,5},{5,6},{6,7},{7,8},{8,9},{9,10},{10,1... | collective-permute-start | bytes 13832 | tf_op jit(solution)/shard_map/ppermute | solution.py:15
  502.4 8.6 %collective-permute-start.19 = (f32[3,4,24,4]{3,2,1,0:T(8,128)S(1)}, f32[3,4,24,4]{3,2,1,0:T(8,128)S(1)}, u32[]{:S(2)}, u32[]{:S(2)}) collective-permute-start(f32[3,4,24,4]{3,2,1,0:T(8,128)S(1)} %get-tuple-element.233), channel_id=1, source_target_pairs={{1,0},{2,1},{3,2},{4,3},{5,4},{6,5},{7,6},{8,7},{9,8},{10,9},{11,1... | collective-permute-start | bytes 13832 | tf_op jit(solution)/shard_map/ppermute | solution.py:18
  522.5 8.7 %collective-permute-start.20 = (f32[6,4,4,128]{3,2,1,0:T(4,128)S(1)}, f32[6,4,4,128]{3,2,1,0:T(4,128)S(1)}, u32[]{:S(2)}, u32[]{:S(2)}) collective-permute-start(f32[6,4,4,128]{3,2,1,0:T(4,128)S(1)} %get-tuple-element.218), channel_id=1, source_target_pairs={{0,16},{16,32},{32,48},{48,64},{64,80},{80,96},{96,112},{112,128},... | collective-permute-start | bytes 147464 | tf_op jit(solution)/shard_map/ppermute | solution.py:15
  538.6 10.0 %collective-permute-start.23 = (f32[6,4,24,4]{3,2,1,0:T(8,128)S(1)}, f32[6,4,24,4]{3,2,1,0:T(8,128)S(1)}, u32[]{:S(2)}, u32[]{:S(2)}) collective-permute-start(f32[6,4,24,4]{3,2,1,0:T(8,128)S(1)} %get-tuple-element.187), channel_id=1, source_target_pairs={{1,0},{2,1},{3,2},{4,3},{5,4},{6,5},{7,6},{8,7},{9,8},{10,9},{11,1... | collective-permute-start | bytes 27656 | tf_op jit(solution)/shard_map/ppermute | solution.py:18
  617.4 9.7 %collective-permute-start.31 = (f32[6,4,24,4]{3,2,1,0:T(8,128)S(1)}, f32[6,4,24,4]{3,2,1,0:T(8,128)S(1)}, u32[]{:S(2)}, u32[]{:S(2)}) collective-permute-start(f32[6,4,24,4]{3,2,1,0:T(8,128)S(1)} %get-tuple-element.167), channel_id=1, source_target_pairs={{1,0},{2,1},{3,2},{4,3},{5,4},{6,5},{7,6},{8,7},{9,8},{10,9},{11,1... | collective-permute-start | bytes 27656 | tf_op jit(solution)/shard_map/ppermute | solution.py:18
  (265 other events, 1059.7 us)
where the time goes:
time: 660 us; the launch traced here: 647 us
  other arithmetic  296 us (45%)
  starting transfers between devices  184 us (28%)
  waiting for transfers between devices  104 us (16%)
  local copies, waits for them, and re-layouts  57.1 us (9%)
    scatter-add x4, other arithmetic, inject(): field.at[layer, safe_x, safe_y]  124 us
    ppermute x32, starting transfers between devices, padded_2(): lax.ppermute(lax.slice_in_dim(block, block.shape[dim] - width, None, axis...  107 us
    ppermute x32, waiting for transfers between devices, padded_2(): lax.ppermute(lax.slice_in_dim(block, 0, width, axis=dim), axis, backward)  92.4 us
    unnamed x41, other arithmetic  84.5 us
    ppermute x32, starting transfers between devices, padded_2(): lax.ppermute(lax.slice_in_dim(block, 0, width, axis=dim), axis, backward)  76.9 us
    slice x115, local copies, waits for them, and re-layouts, shift_diff(): lax.slice_in_dim(field, first, first + length, axis=axis)  40.1 us
    sub x10, other arithmetic, shards(): adj_vel = [adj_vel[i] - step_dt * buoy * div[i] for i in range(3)]  32.4 us
    add x10, other arithmetic, shards(): vel = [vel[i] + step_dt * buoy * div[i] for i in range(3)]  31.1 us
  transfers between devices with their start and end apart: 64, of which 34 were waited for; matrix products, arithmetic and copies ran while one was open for 13% of the time, Pallas kernels for 0%

commit v1 on v0

v1 whole, which is shorter than its diff:
```python
import functools

import jax
import jax.numpy as jnp
from jax import lax
from jax.experimental import pallas as pl
from jax.experimental.pallas import tpu as pltpu
from jax.sharding import PartitionSpec as P

coeffs = (1225.0 / 1024.0, -245.0 / 3072.0, 49.0 / 5120.0, -5.0 / 7168.0)
step_dt = 0.1
MESH = pl.DeviceIdType.MESH

REACH = 4
BASE = 8
LANES = 128
SUB = 8
GROUP = 2 * REACH
PER_TILE = LANES // GROUP

STRESS_ORDER = (3, 6, 7, 4, 8, 5)
XX, XY, XZ, YY, YZ, ZZ = range(6)
X_SIDE, Y_SIDE = (0, 1), (2, 3)


def place_in_grid():
    gx, gy = lax.axis_index("gx"), lax.axis_index("gy")
    return gx, gy, lax.axis_size("gx"), lax.axis_size("gy")


def lane_of(shape):
    return lax.broadcasted_iota(jnp.int32, shape, len(shape) - 1)


def diff_x(buf, field, plus, rows):
    total = None
    for k in range(1, REACH + 1):
        first = BASE + (k if plus else k - 1)
        second = BASE + (1 - k if plus else -k)
        term = coeffs[k - 1] * (
            buf[field, :, first : first + rows, :] - buf[field, :, second : second + rows, :]
        )
        total = term if total is None else total + term
    return total


def shifted_y(field, halo, by):
    if by == 0:
        return field
    lane = lane_of(field.shape)
    if by > 0:
        return pltpu.roll(jnp.where(lane < by, halo, field), LANES - by, 2)
    return pltpu.roll(jnp.where(lane >= LANES + by, halo, field), -by, 2)


def diff_y(field, halo, plus):
    total = None
    for k in range(1, REACH + 1):
        first = k if plus else k - 1
        second = 1 - k if plus else -k
        term = coeffs[k - 1] * (shifted_y(field, halo, first) - shifted_y(field, halo, second))
        total = term if total is None else total + term
    return total


def diff_z(field, plus):
    layers = field.shape[0]
    out = []
    for i in range(layers):
        total = None
        for k in range(1, REACH + 1):
            first = i + (k if plus else k - 1)
            second = i + (1 - k if plus else -k)
            has_first, has_second = 0 <= first < layers, 0 <= second < layers
            if has_first and has_second:
                term = coeffs[k - 1] * (field[first] - field[second])
            elif has_first:
                term = coeffs[k - 1] * field[first]
            elif has_second:
                term = -coeffs[k - 1] * field[second]
            else:
                continue
            total = term if total is None else total + term
        out.append(jnp.zeros_like(field[0]) if total is None else total)
    return jnp.stack(out)


def pack_edges(fields, out_ref):
    layers, rows = fields[0].shape[:2]
    group = lane_of((SUB, LANES)) // GROUP
    tiles = [f[z, r : r + SUB] for f in fields for z in range(layers) for r in range(0, rows, SUB)]
    for start in range(0, len(tiles), PER_TILE):
        packed = jnp.zeros((SUB, LANES), jnp.float32)
        for j, tile in enumerate(tiles[start : start + PER_TILE]):
            packed = jnp.where(group == j, pltpu.roll(tile, (REACH + GROUP * j) % LANES, 1), packed)
        out_ref[start // PER_TILE] = packed


def unpack_edges(low_ref, high_ref, count, layers, rows):
    low_lane = lane_of((SUB, LANES)) % GROUP < REACH
    merged = [
        jnp.where(low_lane, low_ref[i], high_ref[i]) for i in range(low_ref.shape[0])
    ]
    pieces = []
    for j in range(count * layers * (rows // SUB)):
        back = (LANES - REACH - GROUP * (j % PER_TILE)) % LANES
        pieces.append(pltpu.roll(merged[j // PER_TILE], back, 1))
    per_layer = rows // SUB
    halos = []
    for f in range(count):
        halo_layers = []
        for z in range(layers):
            at = (f * layers + z) * per_layer
            halo_layers.append(jnp.concatenate(pieces[at : at + per_layer], axis=0))
        halos.append(jnp.stack(halo_layers))
    return halos


class Exchange:
    def __init__(self, kind, buf, packed, landed, send_sem, recv_sem, rows):
        self.kind, self.buf, self.packed, self.landed = kind, buf, packed, landed
        self.send_sem, self.recv_sem, self.rows = send_sem, recv_sem, rows

    def copies(self):
        gx, gy, nx, ny = place_in_grid()
        kind, end = self.kind, BASE + self.rows

        def rows_of(at):
            return self.buf.at[pl.ds(0, 3), :, pl.ds(at, REACH), :]

        def copy(side, src, dst, axis, to):
            return pltpu.make_async_remote_copy(
                src_ref=src,
                dst_ref=dst,
                send_sem=self.send_sem.at[kind, side],
                recv_sem=self.recv_sem.at[kind, side],
                device_id={axis: to},
                device_id_type=MESH,
            )

        return (
            (gx > 0, gx < nx - 1, copy(0, rows_of(BASE), rows_of(end), "gx", lax.rem(gx + nx - 1, nx))),
            (gx < nx - 1, gx > 0, copy(1, rows_of(end - REACH), rows_of(BASE - REACH), "gx", lax.rem(gx + 1, nx))),
            (gy > 0, gy < ny - 1, copy(2, self.packed.at[kind], self.landed.at[kind, 1], "gy", lax.rem(gy + ny - 1, ny))),
            (gy < ny - 1, gy > 0, copy(3, self.packed.at[kind], self.landed.at[kind, 0], "gy", lax.rem(gy + 1, ny))),
        )

    def start(self):
        for goes, _, copy in self.copies():
            pl.when(goes)(copy.start)

    def wait_recv(self):
        for _, arrives, copy in self.copies():
            pl.when(arrives)(copy.wait_recv)

    def wait_send(self):
        for goes, _, copy in self.copies():
            pl.when(goes)(copy.wait_send)


def own(buf, field, rows):
    return buf[field, :, BASE : BASE + rows, :]


def put(buf, field, rows, value):
    buf[field, :, BASE : BASE + rows, :] = value


def divergence(buf, halos, rows):
    sxy, syy, syz = (own(buf, i, rows) for i in (XY, YY, YZ))
    sxz, szz = own(buf, XZ, rows), own(buf, ZZ, rows)
    return (
        diff_x(buf, XX, True, rows) + diff_y(sxy, halos[0], False) + diff_z(sxz, False),
        diff_x(buf, XY, False, rows) + diff_y(syy, halos[1], True) + diff_z(syz, False),
        diff_x(buf, XZ, False, rows) + diff_y(syz, halos[2], False) + diff_z(szz, True),
    )


def strains(buf, halos, rows):
    vx, vy, vz = (own(buf, i, rows) for i in range(3))
    return (
        diff_x(buf, 0, False, rows),
        diff_y(vy, halos[1], False),
        diff_z(vz, False),
        diff_y(vx, halos[0], True) + diff_x(buf, 1, True, rows),
        diff_z(vx, True) + diff_x(buf, 2, True, rows),
        diff_z(vy, True) + diff_y(vz, halos[2], True),
    )


def log2(n):
    assert n > 0 and n & (n - 1) == 0
    return n.bit_length() - 1


def injections(cells_ref, traces_ref, out_ref, dims):
    layers, rows, nx_cells, ny_cells = dims
    gx, gy, _, _ = place_in_grid()
    steps, count = traces_ref.shape
    cells = cells_ref[...]
    layer = lax.shift_right_logical(cells, jnp.int32(log2(nx_cells * ny_cells)))
    at_x = (lax.shift_right_logical(cells, jnp.int32(log2(ny_cells))) & (nx_cells - 1)) - gx * rows
    at_y = (cells & (ny_cells - 1)) - gy * LANES
    here = (at_x >= 0) & (at_x < rows)
    row = jnp.where(here, layer * rows + at_x, -1)
    total = layers * rows
    row_hit = lax.broadcasted_iota(jnp.int32, (total, count), 0) == row
    lane_hit = lax.broadcasted_iota(jnp.int32, (LANES, count), 0) == at_y
    lanes = jnp.where(lane_hit, 1.0, 0.0).astype(jnp.bfloat16)
    for t in range(steps):
        rest = traces_ref[t : t + 1, :]
        field = None
        for _ in range(3):
            piece = rest.astype(jnp.bfloat16).astype(jnp.float32)
            rest = rest - piece
            spread = jnp.where(row_hit, piece, 0.0).astype(jnp.bfloat16)
            part = lax.dot_general(
                spread, lanes, (((1,), (1,)), ((), ())), preferred_element_type=jnp.float32
            )
            field = part if field is None else field + part
        out_ref[t] = (step_dt * field).reshape(layers, rows, LANES)


def kernel(
    dims,
    fwd_hbm, adj_hbm, labels_hbm, table_ref, src_ref, wav_ref, rec_ref, res_ref,
    out_hbm, gl_hbm, gm_hbm,
    fs, fv, aq, au, labels, mats, inj_f, inj_a, e_all, f_all, grads,
    packed, landed, in_sem, out_sem, send_sem, recv_sem,
):
    layers, rows = dims[0], dims[1]
    gx, gy, nx, ny = place_in_grid()
    steps = wav_ref.shape[0]

    edge = jnp.zeros((3, layers, REACH, LANES), jnp.float32)
    for buf in (fs, fv, aq, au):
        buf[0:3, :, BASE - REACH : BASE, :] = edge
        buf[0:3, :, BASE + rows : BASE + rows + REACH, :] = edge
    landed[...] = jnp.zeros_like(landed)

    barrier = pltpu.get_barrier_semaphore()
    for axis, here, size in (("gx", gx, nx), ("gy", gy, ny)):
        for to in (lax.rem(here + size - 1, size), lax.rem(here + 1, size)):
            pl.semaphore_signal(barrier, inc=1, device_id={axis: to}, device_id_type=MESH)

    loads = []

    def load(src, dst):
        copy = pltpu.make_async_copy(src, dst, in_sem.at[len(loads)])
        copy.start()
        loads.append(copy)

    own_rows = pl.ds(BASE, rows)
    for place, number in enumerate(STRESS_ORDER):
        load(fwd_hbm.at[number], fs.at[place, :, own_rows, :])
    load(adj_hbm.at[pl.ds(0, 3)], au.at[:, :, own_rows, :])
    first = len(loads)
    load(fwd_hbm.at[pl.ds(0, 3)], fv.at[:, :, own_rows, :])
    for place, number in enumerate(STRESS_ORDER):
        load(adj_hbm.at[number], aq.at[place, :, own_rows, :])
    load(labels_hbm, labels)

    def exchange(kind, buf):
        return Exchange(kind, buf, packed, landed, send_sem, recv_sem, rows)

    ex_s, ex_v, ex_u, ex_q = (exchange(i, b) for i, b in enumerate((fs, fv, au, aq)))

    def halos(ex):
        return unpack_edges(landed.at[ex.kind, 0], landed.at[ex.kind, 1], 3, layers, rows)

    for copy in loads[:first]:
        copy.wait()
    pack_edges([own(fs, i, rows) for i in (XY, YY, YZ)], packed.at[0])
    pack_edges([own(au, i, rows) for i in range(3)], packed.at[2])
    pl.semaphore_wait(barrier, 4)
    ex_s.start()
    ex_u.start()

    injections(src_ref, wav_ref, inj_f, dims)
    injections(rec_ref, res_ref, inj_a, dims)
    for copy in loads[first:]:
        copy.wait()
    label = labels[...]
    picked = []
    for prop in range(3):
        value = jnp.full(label.shape, table_ref[prop, 0])
        for phase in range(1, table_ref.shape[1]):
            value = jnp.where(label == phase, table_ref[prop, phase], value)
        picked.append(value)
    mats[0] = step_dt * picked[0]
    mats[1] = step_dt * picked[1]
    mats[2] = step_dt / picked[2]

    def stress_step(buf, strain, sign):
        exx, eyy, ezz, exy, exz, eyz = strain
        lam, shear = mats[0], mats[1]
        base, twice = lam * (exx + eyy + ezz), 2.0 * shear
        for place, inc in (
            (XX, base + twice * exx),
            (XY, shear * exy),
            (XZ, shear * exz),
            (YY, base + twice * eyy),
            (YZ, shear * eyz),
            (ZZ, base + twice * ezz),
        ):
            put(buf, place, rows, own(buf, place, rows) + sign * inc)

    def velocity_step(buf, div, sign, extra):
        buoy = mats[2]
        for i in range(3):
            new = own(buf, i, rows) + sign * (buoy * div[i])
            put(buf, i, rows, new + extra if i == 2 else new)

    def step(t, _):
        ex_s.wait_recv()
        div = divergence(fs, halos(ex_s), rows)
        pl.when(t > 0)(ex_v.wait_send)
        velocity_step(fv, div, 1.0, inj_f[t])
        pack_edges([own(fv, i, rows) for i in range(3)], packed.at[1])
        ex_v.start()
        ex_u.wait_recv()
        strain = strains(au, halos(ex_u), rows)
        for i in range(6):
            f_all[t, i] = strain[i]
        pl.when(t > 0)(ex_q.wait_send)
        stress_step(aq, strain, -1.0)
        pack_edges([own(aq, i, rows) for i in (XY, YY, YZ)], packed.at[3])
        ex_q.start()
        ex_v.wait_recv()
        strain = strains(fv, halos(ex_v), rows)
        for i in range(6):
            e_all[t, i] = strain[i]
        ex_s.wait_send()

        @pl.when(t < steps - 1)
        def _():
            stress_step(fs, [e_all[t, i] for i in range(6)], 1.0)
            pack_edges([own(fs, i, rows) for i in (XY, YY, YZ)], packed.at[0])
            ex_s.start()

        ex_q.wait_recv()
        div = divergence(aq, halos(ex_q), rows)
        ex_u.wait_send()
        velocity_step(au, div, -1.0, inj_a[t])

        @pl.when(t < steps - 1)
        def _():
            pack_edges([own(au, i, rows) for i in range(3)], packed.at[2])
            ex_u.start()

        return 0

    lax.fori_loop(0, steps, step, 0)
    ex_v.wait_send()
    ex_q.wait_send()

    stores = []

    def store(src, dst):
        copy = pltpu.make_async_copy(src, dst, out_sem.at[len(stores)])
        copy.start()
        stores.append(copy)

    store(au.at[:, :, own_rows, :], out_hbm.at[pl.ds(0, 3)])
    for place, number in enumerate(STRESS_ORDER):
        store(aq.at[place, :, own_rows, :], out_hbm.at[number])

    grad_l = grad_m = None
    for t in range(steps):
        e = [e_all[steps - 1 - t, i] for i in range(6)]
        f = [f_all[t, i] for i in range(6)]
        more_l = (e[0] + e[1] + e[2]) * (f[0] + f[1] + f[2])
        more_m = 2.0 * (e[0] * f[0] + e[1] * f[1] + e[2] * f[2])
        more_m = more_m + e[3] * f[3] + e[4] * f[4] + e[5] * f[5]
        grad_l = more_l if grad_l is None else grad_l + more_l
        grad_m = more_m if grad_m is None else grad_m + more_m
    grads[0] = step_dt * grad_l
    grads[1] = step_dt * grad_m
    store(grads.at[0], gl_hbm)
    store(grads.at[1], gm_hbm)
    for copy in stores:
        copy.wait()


def shards(fwd, adj, labels, table, src, wav, rec, res):
    _, layers, rows, lanes = fwd.shape
    assert lanes == LANES and rows % SUB == 0
    nx_cells, ny_cells = rows * lax.axis_size("gx"), lanes * lax.axis_size("gy")
    steps = wav.shape[0]
    dims = (layers, rows, nx_cells, ny_cells)
    tiles = -(-3 * layers * (rows // SUB) // PER_TILE)
    padded = rows + 2 * BASE
    f32 = jnp.float32
    block = (layers, rows, lanes)
    hbm = pl.BlockSpec(memory_space=pl.ANY)
    vmem = pl.BlockSpec(memory_space=pltpu.VMEM)
    smem = pl.BlockSpec(memory_space=pltpu.SMEM)
    return pl.pallas_call(
        functools.partial(kernel, dims),
        out_shape=(
            jax.ShapeDtypeStruct(fwd.shape, f32),
            jax.ShapeDtypeStruct(block, f32),
            jax.ShapeDtypeStruct(block, f32),
        ),
        in_specs=[hbm, hbm, hbm, smem, vmem, vmem, vmem, vmem],
        out_specs=(hbm, hbm, hbm),
        scratch_shapes=[
            pltpu.VMEM((6, layers, padded, lanes), f32),
            pltpu.VMEM((3, layers, padded, lanes), f32),
            pltpu.VMEM((6, layers, padded, lanes), f32),
            pltpu.VMEM((3, layers, padded, lanes), f32),
            pltpu.VMEM(block, jnp.int32),
            pltpu.VMEM((3,) + block, f32),
            pltpu.VMEM((steps,) + block, f32),
            pltpu.VMEM((steps,) + block, f32),
            pltpu.VMEM((steps, 6) + block, f32),
            pltpu.VMEM((steps, 6) + block, f32),
            pltpu.VMEM((2,) + block, f32),
            pltpu.VMEM((4, tiles, SUB, LANES), f32),
            pltpu.VMEM((4, 2, tiles, SUB, LANES), f32),
            pltpu.SemaphoreType.DMA((15,)),
            pltpu.SemaphoreType.DMA((9,)),
            pltpu.SemaphoreType.DMA((4, 4)),
            pltpu.SemaphoreType.DMA((4, 4)),
        ],
        compiler_params=pltpu.CompilerParams(
            collective_id=0, has_side_effects=True, vmem_limit_bytes=32 * 1024 * 1024
        ),
    )(fwd, adj, labels, table, src.reshape(1, -1), wav, rec.reshape(1, -1), res)


def solution(mesh):
    state, cells = P(None, None, "gx", "gy"), P(None, "gx", "gy")
    return jax.shard_map(
        shards,
        mesh=mesh,
        in_specs=(state, state, cells, P(), P(), P(), P(), P()),
        out_specs=(state, cells, cells),
        check_vma=False,
    )
```

time: 660 us -> 49.4 us (0.07)
  the two profiles are of different devices: /device:TPU:103 before, /device:TPU:24 now
where the time goes in v1:
time: 49.4 us; the launch traced here: 49 us
  Pallas kernels  40.3 us (82%)
  local copies, waits for them, and re-layouts  8.08 us (16%)
  between operations  0.66 us (1%)
    pallas_call x1, Pallas kernels, shards(): pl.pallas_call(functools.partial(kernel, dims), out_shape=(jax.ShapeDtype...  40.3 us
    unnamed x19, local copies, waits for them, and re-layouts  8.08 us

profile of v1, /device:TPU:24, one launch (start us, length us, event | category | flops | bytes accessed | tf_op | source)
XLA Modules:
  0.0 49.0 jit_solution(14171409041698422181)
XLA Ops:
  0.6 0.0 copy-start.6
  0.6 0.7 %copy-done.6 = f32[3,4]{1,0:T(4,128)S(1)} copy-done((f32[3,4]{1,0:T(4,128)S(1)}, f32[3,4]{1,0:T(4,128)}, u32[]{:S(2)}) %copy-start.6) | copy-done | bytes 72
  1.3 0.0 copy-start
  1.3 1.0 %copy-done = f32[9,4,16,128]{3,2,1,0:T(8,128)S(1)} copy-done((f32[9,4,16,128]{3,2,1,0:T(8,128)S(1)}, f32[9,4,16,128]{3,2,1,0:T(8,128)}, u32[]{:S(2)}) %copy-start) | copy-done | bytes 294936
  2.3 0.0 copy-start.1
  2.3 1.0 %copy-done.1 = f32[9,4,16,128]{3,2,1,0:T(8,128)S(1)} copy-done((f32[9,4,16,128]{3,2,1,0:T(8,128)S(1)}, f32[9,4,16,128]{3,2,1,0:T(8,128)}, u32[]{:S(2)}) %copy-start.1) | copy-done | bytes 294936
  3.2 0.0 copy-start.2
  3.2 0.8 %copy-done.2 = s32[4,16,128]{2,1,0:T(8,128)S(1)} copy-done((s32[4,16,128]{2,1,0:T(8,128)S(1)}, s32[4,16,128]{2,1,0:T(8,128)}, u32[]{:S(2)}) %copy-start.2) | copy-done | bytes 32792
  4.0 0.0 copy-start.3
  4.0 0.7 %copy-done.3 = f32[4,1024]{1,0:T(4,128)S(1)} copy-done((f32[4,1024]{1,0:T(4,128)S(1)}, f32[4,1024]{1,0:T(4,128)}, u32[]{:S(2)}) %copy-start.3) | copy-done | bytes 16408
  4.7 0.0 copy-start.4
  4.7 0.7 %copy-done.4 = f32[4,512]{1,0:T(4,128)S(1)} copy-done((f32[4,512]{1,0:T(4,128)S(1)}, f32[4,512]{1,0:T(4,128)}, u32[]{:S(2)}) %copy-start.4) | copy-done | bytes 8216
  5.4 0.0 copy-start.5
  5.4 0.7 %copy-done.5 = s32[1024]{0:T(1024)S(1)} copy-done((s32[1024]{0:T(1024)S(1)}, s32[1024]{0:T(1024)}, u32[]{:S(2)}) %copy-start.5) | copy-done | bytes 4120
  6.1 0.0 copy-start.7
  6.1 0.7 %copy-done.7 = s32[512]{0:T(512)S(1)} copy-done((s32[512]{0:T(512)S(1)}, s32[512]{0:T(512)}, u32[]{:S(2)}) %copy-start.7) | copy-done | bytes 2072
  6.8 40.3 %shard_map.103 = (f32[9,4,16,128]{3,2,1,0:T(8,128)S(1)}, f32[4,16,128]{2,1,0:T(8,128)S(1)}, f32[4,16,128]{2,1,0:T(8,128)S(1)}) custom-call(f32[9,4,16,128]{3,2,1,0:T(8,128)S(1)} %copy-done, f32[9,4,16,128]{3,2,1,0:T(8,128)S(1)} %copy-done.1, s32[4,16,128]{2,1,0:T(8,128)S(1)} %copy-done.2, f32[3,4]{1,0:T(4,128)S(1)} %copy-done.6, s32[1,512]{1,0:T(1,128)S(1)} %bitcast.3, ...), custom_call_target="tpu_custom_call" | custom-call | tf_op jit(solution)/shard_map/pallas_call | solution.py:398
  47.1 0.7 %copy.14 = f32[9,4,16,128]{3,2,1,0:T(8,128)} copy(f32[9,4,16,128]{3,2,1,0:T(8,128)S(1)} %get-tuple-element.6) | data formatting | bytes 589824
  47.8 0.6 %copy.15 = f32[4,16,128]{2,1,0:T(8,128)} copy(f32[4,16,128]{2,1,0:T(8,128)S(1)} %get-tuple-element.7) | data formatting | bytes 65536
  48.4 0.6 %copy.16 = f32[4,16,128]{2,1,0:T(8,128)} copy(f32[4,16,128]{2,1,0:T(8,128)S(1)} %get-tuple-element.8) | data formatting | bytes 65536
Async XLA Ops:
  0.6 0.7 %copy-start.6 = (f32[3,4]{1,0:T(4,128)S(1)}, f32[3,4]{1,0:T(4,128)}, u32[]{:S(2)}) copy-start(f32[3,4]{1,0:T(4,128)} %table_ref.1) | copy-start | bytes 148
  1.3 1.0 %copy-start = (f32[9,4,16,128]{3,2,1,0:T(8,128)S(1)}, f32[9,4,16,128]{3,2,1,0:T(8,128)}, u32[]{:S(2)}) copy-start(f32[9,4,16,128]{3,2,1,0:T(8,128)} %fwd_hbm.1) | copy-start | bytes 884740
  2.3 1.0 %copy-start.1 = (f32[9,4,16,128]{3,2,1,0:T(8,128)S(1)}, f32[9,4,16,128]{3,2,1,0:T(8,128)}, u32[]{:S(2)}) copy-start(f32[9,4,16,128]{3,2,1,0:T(8,128)} %adj_hbm.1) | copy-start | bytes 884740
  3.2 0.8 %copy-start.2 = (s32[4,16,128]{2,1,0:T(8,128)S(1)}, s32[4,16,128]{2,1,0:T(8,128)}, u32[]{:S(2)}) copy-start(s32[4,16,128]{2,1,0:T(8,128)} %labels_hbm.1) | copy-start | bytes 98308
  4.0 0.7 %copy-start.3 = (f32[4,1024]{1,0:T(4,128)S(1)}, f32[4,1024]{1,0:T(4,128)}, u32[]{:S(2)}) copy-start(f32[4,1024]{1,0:T(4,128)} %res_ref.1) | copy-start | bytes 49156
  4.7 0.7 %copy-start.4 = (f32[4,512]{1,0:T(4,128)S(1)}, f32[4,512]{1,0:T(4,128)}, u32[]{:S(2)}) copy-start(f32[4,512]{1,0:T(4,128)} %wav_ref.1) | copy-start | bytes 24580
  5.4 0.7 %copy-start.5 = (s32[1024]{0:T(1024)S(1)}, s32[1024]{0:T(1024)}, u32[]{:S(2)}) copy-start(s32[1024]{0:T(1024)} %param.14) | copy-start | bytes 12292
  6.1 0.7 %copy-start.7 = (s32[512]{0:T(512)S(1)}, s32[512]{0:T(512)}, u32[]{:S(2)}) copy-start(s32[512]{0:T(512)} %param.12) | copy-start | bytes 6148

commit v2 on v0

v2 whole, which is shorter than its diff:
```python
import functools

import jax
import jax.numpy as jnp
from jax import lax
from jax.experimental import pallas as pl
from jax.experimental.pallas import tpu as pltpu
from jax.sharding import PartitionSpec as P

coeffs = (1225.0 / 1024.0, -245.0 / 3072.0, 49.0 / 5120.0, -5.0 / 7168.0)
step_dt = 0.1
MESH = pl.DeviceIdType.MESH

LAYERS, ROWS, LANES, SUB = 4, 16, 128, 8
REACH = 4
BASE = 16
PADDED = ROWS + 2 * BASE
END = BASE + ROWS

FWD = (3, 6, 7, 4, 8, 5, 0, 1, 2)
ADJ = (0, 1, 2, 3, 6, 7, 4, 8, 5)
FWD_EDGES = tuple(range(9))
ADJ_EDGES = (0, 1, 2, 4, 6, 7)
FWD_CORNERS = (0, 1, 2, 3, 4)
ADJ_CORNERS = (0, 1)


def place_in_grid():
    gx, gy = lax.axis_index("gx"), lax.axis_index("gy")
    return gx, gy, lax.axis_size("gx"), lax.axis_size("gy")


def lane_of(shape):
    return lax.broadcasted_iota(jnp.int32, shape, len(shape) - 1)


def row_of(shape):
    return lax.broadcasted_iota(jnp.int32, shape, len(shape) - 2)


def roll(value, by):
    by %= LANES
    return value if by == 0 else pltpu.roll(value, by, value.ndim - 1)


def weighted(shift, plus):
    total = None
    for k in range(1, REACH + 1):
        first = k if plus else k - 1
        term = coeffs[k - 1] * (shift(first) - shift(first + 1 - 2 * k))
        total = term if total is None else total + term
    return total


def with_x_halo(buf, field, d=0):
    own = buf[field, :, BASE + d : END + d, :]
    after = buf[field, :, END + d : END + d + SUB, :]
    before = buf[field, :, BASE - SUB + d : BASE + d, :]
    halo = jnp.where(row_of(after.shape) < REACH, after, before)
    return jnp.concatenate([own, halo], axis=1)


def diff_x(buf, field, plus, wide):
    if wide:
        return weighted(lambda d: with_x_halo(buf, field, d), plus)
    return weighted(lambda d: buf[field, :, BASE + d : END + d, :], plus)


def diff_y(field, halo, plus):
    lane = lane_of(field.shape)

    def shift(d):
        if d == 0:
            return field
        return roll(jnp.where(lane < d if d > 0 else lane >= LANES + d, halo, field), -d)

    return weighted(shift, plus)


def diff_z(field, plus):
    out = []
    for i in range(LAYERS):
        total = None
        for k in range(1, REACH + 1):
            first = i + (k if plus else k - 1)
            second = first + 1 - 2 * k
            has_first, has_second = 0 <= first < LAYERS, 0 <= second < LAYERS
            if has_first and has_second:
                term = coeffs[k - 1] * (field[first] - field[second])
            elif has_first:
                term = coeffs[k - 1] * field[first]
            elif has_second:
                term = -coeffs[k - 1] * field[second]
            else:
                continue
            total = term if total is None else total + term
        out.append(total)
    return jnp.stack(out)


def strip_x(buf, field, plus):
    return weighted(lambda d: buf[field, BASE + d : END + d, :], plus)


def strip_y(field, plus):
    return weighted(lambda d: roll(field, -d), plus)


def strip_z(field, plus):
    layer = lane_of(field.shape) // 32
    weights = {}
    for k in range(1, REACH + 1):
        first = k if plus else k - 1
        weights[first] = weights.get(first, 0.0) + coeffs[k - 1]
        weights[first + 1 - 2 * k] = weights.get(first + 1 - 2 * k, 0.0) - coeffs[k - 1]
    total = None
    for d, weight in weights.items():
        if abs(d) >= LAYERS:
            continue
        inside = (layer + d >= 0) & (layer + d < LAYERS)
        term = jnp.where(inside, weight, 0.0) * roll(field, -32 * d)
        total = term if total is None else total + term
    return total


def pack_edge(field):
    group = lane_of((SUB, LANES)) // 16
    packed = None
    for z in range(LAYERS):
        for tile in range(2):
            at = 2 * z + tile
            piece = roll(field[z, SUB * tile : SUB * (tile + 1)], 8 + 16 * at)
            packed = piece if packed is None else jnp.where(group == at, piece, packed)
    return packed


def pack_corners(edges, out_ref, slot):
    group = lane_of((SUB, LANES)) // 8 % 4
    top = row_of((SUB, LANES)) < REACH
    for start in range(0, len(edges), 4):
        packed = None
        for g, edge in enumerate(edges[start : start + 4]):
            piece = jnp.where(top, roll(edge, 8 * g - 4), roll(edge, 8 * g - 20))
            packed = piece if packed is None else jnp.where(group == g, piece, packed)
        out_ref[slot, start // 4] = packed


def strip_of(edge, low, high):
    half = lane_of(edge.shape) % 16 < 8
    first, last = jnp.where(half, low, edge), jnp.where(half, edge, high)
    side = lane_of(edge.shape) % 32 < 16
    tiles = [jnp.where(side, first, roll(last, 16)), jnp.where(side, roll(first, -16), last)]
    return jnp.concatenate(tiles, axis=0)


def y_halo_of_edges(low, high):
    merged = jnp.where(lane_of(low.shape) % 16 < 8, low, high)
    return jnp.stack([
        jnp.concatenate([roll(merged, 120 - 32 * z - 16 * tile) for tile in range(2)], axis=0)
        for z in range(LAYERS)
    ])


def y_halo_of_strip(strip):
    merged = jnp.where(lane_of(strip.shape) % 16 < 8, strip, roll(strip, -16))
    return jnp.stack([roll(merged, 120 - 32 * z) for z in range(LAYERS)])


def y_halo_of_corners(corner, g):
    return jnp.stack([roll(corner, 124 - 32 * z - 8 * g) for z in range(LAYERS)])


def strip_rows_of_corners(corner, g):
    side = lane_of(corner.shape) % 32 < 16
    return jnp.where(side, roll(corner, 4 - 8 * g), roll(corner, 20 - 8 * g))


class Chain:
    def __init__(self, refs, deep, shallow, edges, corners):
        (self.buf, self.edge, self.side, self.corner, self.corners_in,
         self.strips, self.send_sem, self.recv_sem) = refs
        self.deep, self.shallow = deep, shallow
        self.edges, self.corner_places = edges, corners

    def copies(self, slot):
        gx, gy, nx, ny = place_in_grid()
        out = []

        def add(dx, dy, src, dst):
            def inside(sx, sy):
                conds = []
                if sx:
                    conds.append(gx > 0 if sx < 0 else gx < nx - 1)
                if sy:
                    conds.append(gy > 0 if sy < 0 else gy < ny - 1)
                return conds[0] if len(conds) == 1 else jnp.logical_and(*conds)

            copy = pltpu.make_async_remote_copy(
                src_ref=src,
                dst_ref=dst,
                send_sem=self.send_sem.at[slot, len(out)],
                recv_sem=self.recv_sem.at[slot, len(out)],
                device_id=(lax.rem(gx + dx + nx, nx), lax.rem(gy + dy + ny, ny)),
                device_id_type=MESH,
            )
            out.append((inside(dx, dy), inside(-dx, -dy), copy))

        for dx in (-1, 1):
            for dy in (-1, 1):
                at = (1 - dx) // 2 * 2 + (1 - dy) // 2
                add(dx, dy, self.corner.at[slot], self.corners_in.at[slot, at])
        for dy in (-1, 1):
            add(0, dy, self.edge.at[slot], self.side.at[slot, (1 - dy) // 2])
        for fields, count in ((self.deep, SUB), (self.shallow, REACH)):
            for dx in (-1, 1):
                src = BASE if dx < 0 else END - count
                dst = END if dx < 0 else BASE - count
                part = pl.ds(fields[0], len(fields))
                add(dx, 0, self.buf.at[slot, part, :, pl.ds(src, count), :],
                    self.buf.at[slot, part, :, pl.ds(dst, count), :])
        return out

    def clear(self):
        for slot in range(2):
            for fields, count in ((self.deep, SUB), (self.shallow, REACH)):
                zero = jnp.zeros((len(fields), LAYERS, count, LANES), jnp.float32)
                part = pl.ds(fields[0], len(fields))
                self.buf[slot, part, :, BASE - count : BASE, :] = zero
                self.buf[slot, part, :, END : END + count, :] = zero
        self.side[...] = jnp.zeros_like(self.side)
        self.corners_in[...] = jnp.zeros_like(self.corners_in)

    def send(self, slot):
        edges = {}
        for i, place in enumerate(self.edges):
            edges[place] = pack_edge(self.own(slot, place))
            self.edge[slot, i] = edges[place]
        pack_corners([edges[place] for place in self.corner_places], self.corner, slot)
        for goes, _, copy in self.copies(slot):
            pl.when(goes)(copy.start)

    def wait_recv(self, slot):
        for _, arrives, copy in self.copies(slot):
            pl.when(arrives)(copy.wait_recv)

    def wait_send(self, slot):
        for goes, _, copy in self.copies(slot):
            pl.when(goes)(copy.wait_send)

    def own(self, slot, place):
        return self.buf[slot, place, :, BASE:END, :]

    def put(self, slot, place, value):
        self.buf[slot, place, :, BASE:END, :] = value

    def strip(self, slot, place):
        i = self.edges.index(place)
        return strip_of(self.edge[slot, i], self.side[slot, 0, i], self.side[slot, 1, i])

    def y_halo(self, slot, place):
        i = self.edges.index(place)
        return y_halo_of_edges(self.side[slot, 0, i], self.side[slot, 1, i])

    def corner_tiles(self, slot):
        shape = (SUB, LANES)
        first, top = lane_of(shape) % 8 < 4, row_of(shape) < REACH
        out = []
        for i in range(self.corner.shape[1]):
            here = [self.corners_in[slot, at, i] for at in range(4)]
            out.append(jnp.where(top, jnp.where(first, here[2], here[3]),
                                 jnp.where(first, here[0], here[1])))
        return out

    def wide_y_halo(self, slot, place, tiles):
        at = self.corner_places.index(place)
        corner = y_halo_of_corners(tiles[at // 4], at % 4)
        return jnp.concatenate([self.y_halo(slot, place), corner], axis=1)

    def set_strip_rows(self, place, strip, tiles):
        at = self.corner_places.index(place)
        rows = strip_rows_of_corners(tiles[at // 4], at % 4)
        self.strips[place, BASE:END, :] = strip
        self.strips[place, BASE - SUB : BASE, :] = rows
        self.strips[place, END : END + SUB, :] = rows


def put_wide(work, place, value):
    work[place, :, BASE:END, :] = value[:, :ROWS]
    work[place, :, END : END + REACH, :] = value[:, ROWS : ROWS + REACH]
    work[place, :, BASE - REACH : BASE, :] = value[:, ROWS + REACH :]


def log2(n):
    assert n > 0 and n & (n - 1) == 0
    return n.bit_length() - 1


def spread(traces_ref, row, lane, rows, store):
    steps, count = traces_ref.shape
    row_hit = lax.broadcasted_iota(jnp.int32, (rows, count), 0) == row
    lane_hit = lax.broadcasted_iota(jnp.int32, (LANES, count), 0) == lane
    lanes = jnp.where(lane_hit, 1.0, 0.0).astype(jnp.bfloat16)
    for t in range(steps):
        rest = traces_ref[t : t + 1, :]
        total = None
        for _ in range(3):
            piece = rest.astype(jnp.bfloat16).astype(jnp.float32)
            rest = rest - piece
            left = jnp.where(row_hit, piece, 0.0).astype(jnp.bfloat16)
            part = lax.dot_general(
                left, lanes, (((1,), (1,)), ((), ())), preferred_element_type=jnp.float32
            )
            total = part if total is None else total + part
        store(t, step_dt * total)


def positions(cells_ref, nx_cells, ny_cells):
    gx, gy, _, _ = place_in_grid()
    cells = cells_ref[...]
    layer = lax.shift_right_logical(cells, jnp.int32(log2(nx_cells * ny_cells)))
    at_x = lax.shift_right_logical(cells, jnp.int32(log2(ny_cells))) & (nx_cells - 1)
    return layer, at_x - gx * ROWS, (cells & (ny_cells - 1)) - gy * LANES


def kernel(
    dims,
    fwd_hbm, adj_hbm, labels_hbm, table_ref, src_ref, wav_ref, rec_ref, res_ref,
    out_hbm, gl_hbm, gm_hbm,
    f_buf, f_edge, f_side, f_corner, f_corners_in, f_strips,
    a_buf, a_edge, a_side, a_corner, a_corners_in, a_strips,
    f_work, a_work, labels, lab, lab_edge, lab_side, mats, mats_s,
    inj_f, inj_s, inj_a, e_all, f_all, grads,
    in_sem, out_sem, f_send, f_recv, a_send, a_recv, l_send, l_recv,
):
    nx_cells, ny_cells = dims
    gx, gy, nx, ny = place_in_grid()
    steps = wav_ref.shape[0]

    fwd = Chain((f_buf, f_edge, f_side, f_corner, f_corners_in, f_strips, f_send, f_recv),
                (0, 1, 2), (3, 4, 5, 6, 7, 8), FWD_EDGES, FWD_CORNERS)
    adj = Chain((a_buf, a_edge, a_side, a_corner, a_corners_in, a_strips, a_send, a_recv),
                (0, 1, 2), (3, 4, 5), ADJ_EDGES, ADJ_CORNERS)

    fwd.clear()
    adj.clear()
    lab[...] = jnp.zeros_like(lab)
    lab_side[...] = jnp.zeros_like(lab_side)
    barrier = pltpu.get_barrier_semaphore()
    around = [(dx, dy) for dx in (-1, 0, 1) for dy in (-1, 0, 1) if dx or dy]
    for dx, dy in around:
        to = (lax.rem(gx + dx + nx, nx), lax.rem(gy + dy + ny, ny))
        pl.semaphore_signal(barrier, inc=1, device_id=to, device_id_type=MESH)

    loads = []

    def load(src, dst):
        copy = pltpu.make_async_copy(src, dst, in_sem.at[len(loads)])
        copy.start()
        loads.append(copy)

    own_rows = pl.ds(BASE, ROWS)
    load(labels_hbm, labels)
    for place, number in enumerate(FWD):
        load(fwd_hbm.at[number], f_buf.at[0, place, :, own_rows, :])
    for place, number in enumerate(ADJ):
        load(adj_hbm.at[number], a_buf.at[0, place, :, own_rows, :])

    loads[0].wait()
    lab[0, :, BASE:END, :] = labels[...].astype(jnp.float32)
    lab_edge[0] = pack_edge(lab[0, :, BASE:END, :])
    lab_copies = []
    for goes, arrives, src, dst, axis, to in (
        (gx > 0, gx < nx - 1, lab.at[0, :, pl.ds(BASE, REACH), :], lab.at[0, :, pl.ds(END, REACH), :], "gx", lax.rem(gx + nx - 1, nx)),
        (gx < nx - 1, gx > 0, lab.at[0, :, pl.ds(END - REACH, REACH), :], lab.at[0, :, pl.ds(BASE - REACH, REACH), :], "gx", lax.rem(gx + 1, nx)),
        (gy > 0, gy < ny - 1, lab_edge, lab_side.at[1], "gy", lax.rem(gy + ny - 1, ny)),
        (gy < ny - 1, gy > 0, lab_edge, lab_side.at[0], "gy", lax.rem(gy + 1, ny)),
    ):
        copy = pltpu.make_async_remote_copy(
            src_ref=src, dst_ref=dst, send_sem=l_send.at[len(lab_copies)],
            recv_sem=l_recv.at[len(lab_copies)], device_id={axis: to}, device_id_type=MESH,
        )
        lab_copies.append((goes, arrives, copy))

    for copy in loads[1:]:
        copy.wait()
    pl.semaphore_wait(barrier, len(around))
    fwd.send(0)
    adj.send(0)
    for goes, _, copy in lab_copies:
        pl.when(goes)(copy.start)

    layer, at_x, at_y = positions(src_ref, nx_cells, ny_cells)
    wide = ROWS + SUB
    here = jnp.where(at_x < 0, at_x + wide, at_x)
    row = jnp.where((at_x >= -REACH) & (at_x < ROWS + REACH), layer * wide + here, -1)

    def store_wide(t, value):
        inj_f[t] = value.reshape(LAYERS, wide, LANES)

    spread(wav_ref, row, at_y, LAYERS * wide, store_wide)
    column = jnp.where((at_y >= -REACH) & (at_y < 0), 32 * layer + 8 + at_y, -1)
    column = jnp.where((at_y >= LANES) & (at_y < LANES + REACH), 32 * layer + 24 + at_y - LANES, column)

    def store_strip(t, value):
        inj_s[t] = value

    spread(wav_ref, at_x, column, ROWS, store_strip)
    layer, at_x, at_y = positions(rec_ref, nx_cells, ny_cells)
    row = jnp.where((at_x >= 0) & (at_x < ROWS), layer * ROWS + at_x, -1)

    def store_own(t, value):
        inj_a[t] = value.reshape(LAYERS, ROWS, LANES)

    spread(res_ref, row, at_y, LAYERS * ROWS, store_own)

    for _, arrives, copy in lab_copies:
        pl.when(arrives)(copy.wait_recv)

    def materials(label, inside, out):
        for prop in range(3):
            value = jnp.full(label.shape, table_ref[prop, 0])
            for phase in range(1, table_ref.shape[1]):
                value = jnp.where(label == phase, table_ref[prop, phase], value)
            value = step_dt * value if prop < 2 else step_dt / value
            out[prop] = jnp.where(inside, value, 0.0)

    shape = (LAYERS, wide, LANES)
    r = row_of(shape)
    inside = (r < ROWS) | ((r < ROWS + REACH) & (gx < nx - 1)) | ((r >= ROWS + REACH) & (gx > 0))
    materials(with_x_halo(lab, 0), inside, mats)
    lane = lane_of((ROWS, LANES))
    column = lane % 16 + jnp.where(lane % 32 < 16, -8, LANES - 8)
    inside = ((column >= 0) | (gy > 0)) & ((column < LANES) | (gy < ny - 1))
    materials(strip_of(lab_edge[0], lab_side[0, 0], lab_side[1, 0]), inside, mats_s)

    def forward_step(t):
        slot = lax.rem(t, 2)
        other = 1 - slot
        buf = f_buf.at[slot]
        fwd.wait_recv(slot)
        tiles = fwd.corner_tiles(slot)
        div = []
        sxx, sxy, sxz, syy, syz, szz, vx, vy, vz = range(9)
        for first, second, third, plus in (
            (sxx, sxy, sxz, 0), (sxy, syy, syz, 1), (sxz, syz, szz, 2)
        ):
            div.append(
                diff_x(buf, first, plus == 0, True)
                + diff_y(with_x_halo(buf, second), fwd.wide_y_halo(slot, second, tiles), plus == 1)
                + diff_z(with_x_halo(buf, third), plus == 2)
            )
        strips = [fwd.strip(slot, place) for place in range(9)]
        for place in (sxx, sxy, sxz):
            fwd.set_strip_rows(place, strips[place], tiles)
        strip_div = [
            strip_x(f_strips, sxx, True) + strip_y(strips[sxy], False) + strip_z(strips[sxz], False),
            strip_x(f_strips, sxy, False) + strip_y(strips[syy], True) + strip_z(strips[syz], False),
            strip_x(f_strips, sxz, False) + strip_y(strips[syz], False) + strip_z(strips[szz], True),
        ]
        pl.when(t > 0)(lambda: fwd.wait_send(other))
        halos = []
        for i in range(3):
            new = with_x_halo(buf, vx + i) + mats[2] * div[i]
            side = strips[vx + i] + mats_s[2] * strip_div[i]
            if i == 2:
                new, side = new + inj_f[t], side + inj_s[t]
            put_wide(f_work, i, new)
            fwd.put(other, vx + i, new[:, :ROWS])
            halos.append(y_halo_of_strip(side))
        v = [fwd.own(other, vx + i) for i in range(3)]
        strain = (
            diff_x(f_work, 0, False, False),
            diff_y(v[1], halos[1], False),
            diff_z(v[2], False),
            diff_y(v[0], halos[0], True) + diff_x(f_work, 1, True, False),
            diff_z(v[0], True) + diff_x(f_work, 2, True, False),
            diff_z(v[1], True) + diff_y(v[2], halos[2], True),
        )
        for i in range(6):
            e_all[t, i] = strain[i]

        @pl.when(t < steps - 1)
        def _():
            lam, shear = mats[0, :, :ROWS], mats[1, :, :ROWS]
            exx, eyy, ezz, exy, exz, eyz = (e_all[t, i] for i in range(6))
            base, twice = lam * (exx + eyy + ezz), 2.0 * shear
            for place, inc in (
                (sxx, base + twice * exx), (sxy, shear * exy), (sxz, shear * exz),
                (syy, base + twice * eyy), (syz, shear * eyz), (szz, base + twice * ezz),
            ):
                fwd.put(other, place, fwd.own(slot, place) + inc)
            fwd.send(other)

    def adjoint_step(t):
        slot = lax.rem(t, 2)
        other = 1 - slot
        buf = a_buf.at[slot]
        adj.wait_recv(slot)
        tiles = adj.corner_tiles(slot)
        vx, vy, vz, sxx, sxy, sxz, syy, syz, szz = range(9)
        u = [with_x_halo(buf, i) for i in range(3)]
        u_halo = [adj.wide_y_halo(slot, i, tiles) for i in range(2)]
        u_own = adj.own(slot, vz)
        exx, eyy, ezz = diff_x(buf, vx, False, True), diff_y(u[1], u_halo[1], False), diff_z(u[2], False)
        exy = diff_y(u[0], u_halo[0], True) + diff_x(buf, vy, True, True)
        exz = diff_z(u[0], True) + diff_x(buf, vz, True, True)
        eyz = diff_z(adj.own(slot, vy), True) + diff_y(u_own, adj.y_halo(slot, vz), True)
        for i, value in enumerate((exx, eyy, ezz, exy, exz)):
            f_all[t, i] = value[:, :ROWS]
        f_all[t, 5] = eyz
        side = [adj.strip(slot, i) for i in range(3)]
        for i in range(2):
            adj.set_strip_rows(i, side[i], tiles)
        side_xx, side_yy, side_zz = strip_x(a_strips, vx, False), strip_y(side[1], False), strip_z(side[2], False)
        side_xy = strip_y(side[0], True) + strip_x(a_strips, vy, True)
        side_yz = strip_z(side[1], True) + strip_y(side[2], True)
        pl.when(t > 0)(lambda: adj.wait_send(other))
        lam, shear = mats[0], mats[1]
        base = lam * (exx + eyy + ezz)
        for i, (place, inc) in enumerate(
            ((sxx, base + 2.0 * shear * exx), (sxy, shear * exy), (sxz, shear * exz))
        ):
            new = with_x_halo(buf, place) - inc
            put_wide(a_work, i, new)
            adj.put(other, place, new[:, :ROWS])
        base, shear = base[:, :ROWS], shear[:, :ROWS]
        for place, inc in (
            (syy, base + 2.0 * shear * eyy[:, :ROWS]),
            (syz, shear * eyz),
            (szz, base + 2.0 * shear * ezz[:, :ROWS]),
        ):
            adj.put(other, place, adj.own(slot, place) - inc)
        lam, shear = mats_s[0], mats_s[1]
        side_inc = {
            sxy: shear * side_xy,
            syy: lam * (side_xx + side_yy + side_zz) + 2.0 * shear * side_yy,
            syz: shear * side_yz,
        }
        halo = {
            place: y_halo_of_strip(adj.strip(slot, place) - inc) for place, inc in side_inc.items()
        }
        new = {place: adj.own(other, place) for place in (sxy, sxz, syy, syz, szz)}
        div = (
            diff_x(a_work, 0, True, False) + diff_y(new[sxy], halo[sxy], False) + diff_z(new[sxz], False),
            diff_x(a_work, 1, False, False) + diff_y(new[syy], halo[syy], True) + diff_z(new[syz], False),
            diff_x(a_work, 2, False, False) + diff_y(new[syz], halo[syz], False) + diff_z(new[szz], True),
        )
        buoy = mats[2, :, :ROWS]
        for i in range(3):
            value = adj.own(slot, i) - buoy * div[i]
            adj.put(other, i, value + inj_a[t] if i == 2 else value)
        pl.when(t < steps - 1)(lambda: adj.send(other))

    def step(t, _):
        forward_step(t)
        adjoint_step(t)
        return 0

    lax.fori_loop(0, steps, step, 0)
    last = (steps - 1) % 2
    fwd.wait_send(last)
    adj.wait_send(last)
    for goes, _, copy in lab_copies:
        pl.when(goes)(copy.wait_send)

    stores = []

    def store(src, dst):
        copy = pltpu.make_async_copy(src, dst, out_sem.at[len(stores)])
        copy.start()
        stores.append(copy)

    for place, number in enumerate(ADJ):
        store(a_buf.at[1 - last, place, :, own_rows, :], out_hbm.at[number])

    grad_l = grad_m = None
    for t in range(steps):
        e = [e_all[steps - 1 - t, i] for i in range(6)]
        f = [f_all[t, i] for i in range(6)]
        more_l = (e[0] + e[1] + e[2]) * (f[0] + f[1] + f[2])
        more_m = 2.0 * (e[0] * f[0] + e[1] * f[1] + e[2] * f[2])
        more_m = more_m + e[3] * f[3] + e[4] * f[4] + e[5] * f[5]
        grad_l = more_l if grad_l is None else grad_l + more_l
        grad_m = more_m if grad_m is None else grad_m + more_m
    grads[0] = step_dt * grad_l
    grads[1] = step_dt * grad_m
    store(grads.at[0], gl_hbm)
    store(grads.at[1], gm_hbm)
    for copy in stores:
        copy.wait()


def shards(fwd, adj, labels, table, src, wav, rec, res):
    assert labels.shape == (LAYERS, ROWS, LANES)
    dims = (ROWS * lax.axis_size("gx"), LANES * lax.axis_size("gy"))
    steps = wav.shape[0]
    f32 = jnp.float32
    block, tile = (LAYERS, ROWS, LANES), (SUB, LANES)
    wide = (LAYERS, ROWS + SUB, LANES)

    def vmem(*shape):
        return pltpu.VMEM(shape, f32)

    def chain(edges, corners, strips):
        return [
            vmem(2, 9, LAYERS, PADDED, LANES),
            vmem(2, edges, *tile),
            vmem(2, 2, edges, *tile),
            vmem(2, corners, *tile),
            vmem(2, 4, corners, *tile),
            vmem(strips, PADDED, LANES),
        ]

    in_hbm = pl.BlockSpec(memory_space=pl.ANY)
    in_vmem = pl.BlockSpec(memory_space=pltpu.VMEM)
    in_smem = pl.BlockSpec(memory_space=pltpu.SMEM)
    dma = pltpu.SemaphoreType.DMA
    return pl.pallas_call(
        functools.partial(kernel, dims),
        out_shape=(
            jax.ShapeDtypeStruct(fwd.shape, f32),
            jax.ShapeDtypeStruct(block, f32),
            jax.ShapeDtypeStruct(block, f32),
        ),
        in_specs=[in_hbm, in_hbm, in_hbm, in_smem, in_vmem, in_vmem, in_vmem, in_vmem],
        out_specs=(in_hbm, in_hbm, in_hbm),
        scratch_shapes=chain(9, 2, 3) + chain(6, 1, 2) + [
            vmem(3, LAYERS, PADDED, LANES),
            vmem(3, LAYERS, PADDED, LANES),
            pltpu.VMEM(block, jnp.int32),
            vmem(1, LAYERS, PADDED, LANES),
            vmem(1, *tile),
            vmem(2, 1, *tile),
            vmem(3, *wide),
            vmem(3, ROWS, LANES),
            vmem(steps, *wide),
            vmem(steps, ROWS, LANES),
            vmem(steps, *block),
            vmem(steps, 6, *block),
            vmem(steps, 6, *block),
            vmem(2, *block),
            dma((19,)), dma((11,)),
            dma((2, 10)), dma((2, 10)), dma((2, 10)), dma((2, 10)),
            dma((4,)), dma((4,)),
        ],
        compiler_params=pltpu.CompilerParams(
            collective_id=0, has_side_effects=True, vmem_limit_bytes=62 * 1024 * 1024
        ),
    )(fwd, adj, labels, table, src.reshape(1, -1), wav, rec.reshape(1, -1), res)


def solution(mesh):
    state, cells = P(None, None, "gx", "gy"), P(None, "gx", "gy")
    return jax.shard_map(
        shards,
        mesh=mesh,
        in_specs=(state, state, cells, P(), P(), P(), P(), P()),
        out_specs=(state, cells, cells),
        check_vma=False,
    )
```

time: 660 us -> 38.7 us (0.06)
  the two profiles are of different devices: /device:TPU:103 before, /device:TPU:24 now
where the time goes in v2:
time: 38.7 us; the launch traced here: 38.4 us
  Pallas kernels  34.6 us (89%)
  local copies, waits for them, and re-layouts  3.09 us (8%)
  between operations  0.65 us (2%)
    pallas_call x1, Pallas kernels, shards(): pl.pallas_call(functools.partial(kernel, dims), out_shape=(jax.ShapeDtype...  34.6 us
    unnamed x7, local copies, waits for them, and re-layouts  3.09 us

profile of v2, /device:TPU:24, one launch (start us, length us, event | category | flops | bytes accessed | tf_op | source)
XLA Modules:
  0.0 38.4 jit_solution(12364732508960180438)
XLA Ops:
  0.6 34.6 %shard_map.103 = (f32[9,4,16,128]{3,2,1,0:T(8,128)}, f32[4,16,128]{2,1,0:T(8,128)}, f32[4,16,128]{2,1,0:T(8,128)}) custom-call(f32[9,4,16,128]{3,2,1,0:T(8,128)} %fwd_hbm.1, f32[9,4,16,128]{3,2,1,0:T(8,128)} %adj_hbm.1, s32[4,16,128]{2,1,0:T(8,128)} %labels_hbm.1, f32[3,4]{1,0:T(4,128)} %table_ref.1, s32[1,512]{1,0:T(1,128)} %bitcast.3, f32[4,512]{1,0:T(4,128)} %wav_ref.1, ...), custom_call_target="tpu_custom_call" | custom-call | tf_op jit(solution)/shard_map/pallas_call | solution.py:618
  35.3 0.0 copy-start.1
  35.3 1.7 %copy.14 = f32[9,4,16,128]{3,2,1,0:T(8,128)} copy(f32[9,4,16,128]{3,2,1,0:T(8,128)} %get-tuple-element.6) | data formatting | bytes 589824
  37.0 0.0 copy-done.1
  37.0 0.0 copy-start
  37.0 0.6 %copy.15 = f32[4,16,128]{2,1,0:T(8,128)} copy(f32[4,16,128]{2,1,0:T(8,128)S(1)} %copy-done.1) | data formatting | bytes 65536
  37.6 0.2 copy-done
  37.8 0.6 %copy.16 = f32[4,16,128]{2,1,0:T(8,128)} copy(f32[4,16,128]{2,1,0:T(8,128)S(1)} %copy-done) | data formatting | bytes 65536
Async XLA Ops:
  35.3 1.7 %copy-start.1 = (f32[4,16,128]{2,1,0:T(8,128)S(1)}, f32[4,16,128]{2,1,0:T(8,128)}, u32[]{:S(2)}) copy-start(f32[4,16,128]{2,1,0:T(8,128)} %get-tuple-element.7) | copy-start | bytes 98308
  37.0 0.8 %copy-start = (f32[4,16,128]{2,1,0:T(8,128)S(1)}, f32[4,16,128]{2,1,0:T(8,128)}, u32[]{:S(2)}) copy-start(f32[4,16,128]{2,1,0:T(8,128)} %get-tuple-element.8) | copy-start | bytes 98308

commit v3 on v2

--- a/solution.py
+++ b/solution.py
@@ -324,8 +324,9 @@
 
 def kernel(
     dims,
-    fwd_hbm, adj_hbm, labels_hbm, table_ref, src_ref, wav_ref, rec_ref, res_ref,
-    out_hbm, gl_hbm, gm_hbm,
+    fwd_hbm, adj_hbm, labels_hbm, table_hbm, src_hbm, wav_hbm, rec_hbm, res_hbm,
+    out_ref, gl_ref, gm_ref,
+    table_ref, src_ref, wav_ref, rec_ref, res_ref,
     f_buf, f_edge, f_side, f_corner, f_corners_in, f_strips,
     a_buf, a_edge, a_side, a_corner, a_corners_in, a_strips,
     f_work, a_work, labels, lab, lab_edge, lab_side, mats, mats_s,
@@ -341,6 +342,26 @@
     adj = Chain((a_buf, a_edge, a_side, a_corner, a_corners_in, a_strips, a_send, a_recv),
                 (0, 1, 2), (3, 4, 5), ADJ_EDGES, ADJ_CORNERS)
 
+    loads = []
+
+    def load(src, dst):
+        copy = pltpu.make_async_copy(src, dst, in_sem.at[len(loads)])
+        copy.start()
+        loads.append(copy)
+
+    own_rows = pl.ds(BASE, ROWS)
+    load(labels_hbm, labels)
+    for place, number in enumerate(FWD):
+        load(fwd_hbm.at[number], f_buf.at[0, place, :, own_rows, :])
+    for place, number in enumerate(ADJ):
+        load(adj_hbm.at[number], a_buf.at[0, place, :, own_rows, :])
+    first = len(loads)
+    for src, dst in (
+        (table_hbm, table_ref), (src_hbm, src_ref), (wav_hbm, wav_ref),
+        (rec_hbm, rec_ref), (res_hbm, res_ref),
+    ):
+        load(src, dst)
+
     fwd.clear()
     adj.clear()
     lab[...] = jnp.zeros_like(lab)
@@ -350,20 +371,6 @@
     for dx, dy in around:
         to = (lax.rem(gx + dx + nx, nx), lax.rem(gy + dy + ny, ny))
         pl.semaphore_signal(barrier, inc=1, device_id=to, device_id_type=MESH)
-
-    loads = []
-
-    def load(src, dst):
-        copy = pltpu.make_async_copy(src, dst, in_sem.at[len(loads)])
-        copy.start()
-        loads.append(copy)
-
-    own_rows = pl.ds(BASE, ROWS)
-    load(labels_hbm, labels)
-    for place, number in enumerate(FWD):
-        load(fwd_hbm.at[number], f_buf.at[0, place, :, own_rows, :])
-    for place, number in enumerate(ADJ):
-        load(adj_hbm.at[number], a_buf.at[0, place, :, own_rows, :])
 
     loads[0].wait()
     lab[0, :, BASE:END, :] = labels[...].astype(jnp.float32)
@@ -381,7 +388,7 @@
         )
         lab_copies.append((goes, arrives, copy))
 
-    for copy in loads[1:]:
+    for copy in loads[1:first]:
         copy.wait()
     pl.semaphore_wait(barrier, len(around))
     fwd.send(0)
@@ -389,6 +396,8 @@
     for goes, _, copy in lab_copies:
         pl.when(goes)(copy.start)
 
+    for copy in loads[first:]:
+        copy.wait()
     layer, at_x, at_y = positions(src_ref, nx_cells, ny_cells)
     wide = ROWS + SUB
     here = jnp.where(at_x < 0, at_x + wide, at_x)
@@ -434,7 +443,7 @@
     materials(strip_of(lab_edge[0], lab_side[0, 0], lab_side[1, 0]), inside, mats_s)
 
     def forward_step(t):
-        slot = lax.rem(t, 2)
+        slot = t % 2
         other = 1 - slot
         buf = f_buf.at[slot]
         fwd.wait_recv(slot)
@@ -457,7 +466,8 @@
             strip_x(f_strips, sxy, False) + strip_y(strips[syy], True) + strip_z(strips[syz], False),
             strip_x(f_strips, sxz, False) + strip_y(strips[syz], False) + strip_z(strips[szz], True),
         ]
-        pl.when(t > 0)(lambda: fwd.wait_send(other))
+        if t > 0:
+            fwd.wait_send(other)
         halos = []
         for i in range(3):
             new = with_x_halo(buf, vx + i) + mats[2] * div[i]
@@ -479,10 +489,9 @@
         for i in range(6):
             e_all[t, i] = strain[i]
 
-        @pl.when(t < steps - 1)
-        def _():
+        if t < steps - 1:
             lam, shear = mats[0, :, :ROWS], mats[1, :, :ROWS]
-            exx, eyy, ezz, exy, exz, eyz = (e_all[t, i] for i in range(6))
+            exx, eyy, ezz, exy, exz, eyz = strain
             base, twice = lam * (exx + eyy + ezz), 2.0 * shear
             for place, inc in (
                 (sxx, base + twice * exx), (sxy, shear * exy), (sxz, shear * exz),
@@ -492,7 +501,7 @@
             fwd.send(other)
 
     def adjoint_step(t):
-        slot = lax.rem(t, 2)
+        slot = t % 2
         other = 1 - slot
         buf = a_buf.at[slot]
         adj.wait_recv(slot)
@@ -514,7 +523,8 @@
         side_xx, side_yy, side_zz = strip_x(a_strips, vx, False), strip_y(side[1], False), strip_z(side[2], False)
         side_xy = strip_y(side[0], True) + strip_x(a_strips, vy, True)
         side_yz = strip_z(side[1], True) + strip_y(side[2], True)
-        pl.when(t > 0)(lambda: adj.wait_send(other))
+        if t > 0:
+            adj.wait_send(other)
         lam, shear = mats[0], mats[1]
         base = lam * (exx + eyy + ezz)
         for i, (place, inc) in enumerate(
@@ -549,29 +559,21 @@
         for i in range(3):
             value = adj.own(slot, i) - buoy * div[i]
             adj.put(other, i, value + inj_a[t] if i == 2 else value)
-        pl.when(t < steps - 1)(lambda: adj.send(other))
-
-    def step(t, _):
+        if t < steps - 1:
+            adj.send(other)
+
+    for t in range(steps):
         forward_step(t)
         adjoint_step(t)
-        return 0
-
-    lax.fori_loop(0, steps, step, 0)
+
     last = (steps - 1) % 2
     fwd.wait_send(last)
     adj.wait_send(last)
     for goes, _, copy in lab_copies:
         pl.when(goes)(copy.wait_send)
 
-    stores = []
-
-    def store(src, dst):
-        copy = pltpu.make_async_copy(src, dst, out_sem.at[len(stores)])
-        copy.start()
-        stores.append(copy)
-
     for place, number in enumerate(ADJ):
-        store(a_buf.at[1 - last, place, :, own_rows, :], out_hbm.at[number])
+        out_ref[number] = adj.own(1 - last, place)
 
     grad_l = grad_m = None
     for t in range(steps):
@@ -582,11 +584,16 @@
         more_m = more_m + e[3] * f[3] + e[4] * f[4] + e[5] * f[5]
         grad_l = more_l if grad_l is None else grad_l + more_l
         grad_m = more_m if grad_m is None else grad_m + more_m
-    grads[0] = step_dt * grad_l
-    grads[1] = step_dt * grad_m
-    store(grads.at[0], gl_hbm)
-    store(grads.at[1], gm_hbm)
-    for copy in stores:
+    gl_ref[...] = step_dt * grad_l
+    gm_ref[...] = step_dt * grad_m
+
+
+def hand_over(*refs):
+    sem = refs[-1]
+    copies = [pltpu.make_async_copy(refs[i], refs[3 + i], sem.at[i]) for i in range(3)]
+    for copy in copies:
+        copy.start()
+    for copy in copies:
         copy.wait()
 
 
@@ -613,18 +620,27 @@
 
     in_hbm = pl.BlockSpec(memory_space=pl.ANY)
     in_vmem = pl.BlockSpec(memory_space=pltpu.VMEM)
-    in_smem = pl.BlockSpec(memory_space=pltpu.SMEM)
     dma = pltpu.SemaphoreType.DMA
-    return pl.pallas_call(
+    operands = [
+        pltpu.with_memory_space_constraint(x, pltpu.HBM)
+        for x in (fwd, adj, labels, table, src.reshape(1, -1), wav, rec.reshape(1, -1), res)
+    ]
+    results = pl.pallas_call(
         functools.partial(kernel, dims),
         out_shape=(
-            jax.ShapeDtypeStruct(fwd.shape, f32),
-            jax.ShapeDtypeStruct(block, f32),
-            jax.ShapeDtypeStruct(block, f32),
+            pltpu.VMEM(fwd.shape, f32),
+            pltpu.VMEM(block, f32),
+            pltpu.VMEM(block, f32),
         ),
-        in_specs=[in_hbm, in_hbm, in_hbm, in_smem, in_vmem, in_vmem, in_vmem, in_vmem],
-        out_specs=(in_hbm, in_hbm, in_hbm),
-        scratch_shapes=chain(9, 2, 3) + chain(6, 1, 2) + [
+        in_specs=[in_hbm] * 8,
+        out_specs=(in_vmem, in_vmem, in_vmem),
+        scratch_shapes=[
+            pltpu.SMEM(table.shape, f32),
+            pltpu.VMEM((1,) + src.shape, jnp.int32),
+            vmem(*wav.shape),
+            pltpu.VMEM((1,) + rec.shape, jnp.int32),
+            vmem(*res.shape),
+        ] + chain(9, 2, 3) + chain(6, 1, 2) + [
             vmem(3, LAYERS, PADDED, LANES),
             vmem(3, LAYERS, PADDED, LANES),
             pltpu.VMEM(block, jnp.int32),
@@ -639,14 +655,25 @@
             vmem(steps, 6, *block),
             vmem(steps, 6, *block),
             vmem(2, *block),
-            dma((19,)), dma((11,)),
+            dma((24,)), dma((11,)),
             dma((2, 10)), dma((2, 10)), dma((2, 10)), dma((2, 10)),
             dma((4,)), dma((4,)),
         ],
         compiler_params=pltpu.CompilerParams(
-            collective_id=0, has_side_effects=True, vmem_limit_bytes=62 * 1024 * 1024
+            collective_id=0, has_side_effects=True, vmem_limit_bytes=40 * 1024 * 1024
         ),
-    )(fwd, adj, labels, table, src.reshape(1, -1), wav, rec.reshape(1, -1), res)
+    )(*operands)
+    return pl.pallas_call(
+        hand_over,
+        out_shape=(
+            pltpu.HBM(fwd.shape, f32),
+            pltpu.HBM(block, f32),
+            pltpu.HBM(block, f32),
+        ),
+        in_specs=[in_hbm] * 3,
+        out_specs=(in_hbm,) * 3,
+        scratch_shapes=[dma((3,))],
+    )(*(pltpu.with_memory_space_constraint(r, pltpu.VMEM) for r in results))
 
 
 def solution(mesh):

time: 38.7 us -> 34.4 us (0.89)
  local copies, waits for them, and re-layouts: 3.09 us -> 0 us
  Pallas kernels: 34.6 us -> 33.5 us
    unnamed x7 -> x0, local copies, waits for them, and re-layouts: 3.09 us -> none
    pallas_call x1 -> x2, Pallas kernels: 34.6 us -> 33.5 us  [the longest x1 32.8 us: shards(): pl.pallas_call(functools.partial(kernel, dims), out_shape=(pltpu.VMEM(fwd...]
where the time goes in v3:
time: 34.4 us; the launch traced here: 34.2 us
  Pallas kernels  33.5 us (97%)
  between operations  0.64 us (2%)
    pallas_call x1, Pallas kernels, shards(): pl.pallas_call(functools.partial(kernel, dims), out_shape=(pltpu.VMEM(fwd...  32.8 us
    pallas_call x1, Pallas kernels, shards(): pl.pallas_call(hand_over, out_shape=(pltpu.HBM(fwd.shape, f32), pltpu.HBM...  0.75 us

profile of v3, /device:TPU:24, one launch (start us, length us, event | category | flops | bytes accessed | tf_op | source)
XLA Modules:
  0.0 34.2 jit_solution(1677223146499931899)
XLA Ops:
  0.6 32.8 %shard_map.103 = (f32[9,4,16,128]{3,2,1,0:T(8,128)S(1)}, f32[4,16,128]{2,1,0:T(8,128)S(1)}, f32[4,16,128]{2,1,0:T(8,128)S(1)}) custom-call(f32[9,4,16,128]{3,2,1,0:T(8,128)} %fwd_hbm.1, f32[9,4,16,128]{3,2,1,0:T(8,128)} %adj_hbm.1, s32[4,16,128]{2,1,0:T(8,128)} %labels_hbm.1, f32[3,4]{1,0:T(4,128)} %table_hbm.1, s32[1,512]{1,0:T(1,128)} %bitcast.3, ...), custom_call_target="tpu_custom_call" | custom-call | tf_op jit(solution)/shard_map/pallas_call | solution.py:628
  33.4 0.8 %shard_map.104 = (f32[9,4,16,128]{3,2,1,0:T(8,128)}, f32[4,16,128]{2,1,0:T(8,128)}, f32[4,16,128]{2,1,0:T(8,128)}) custom-call(f32[9,4,16,128]{3,2,1,0:T(8,128)S(1)} %get-tuple-element.6.refs_0_, f32[4,16,128]{2,1,0:T(8,128)S(1)} %get-tuple-element.7.refs_1_, f32[4,16,128]{2,1,0:T(8,128)S(1)} %get-tuple-element.8.refs_2_), custom_call_target="tpu_custom_call" | custom-call | tf_op jit(solution)/shard_map/pallas_call | solution.py:666

commit v4 on v3

--- a/solution.py
+++ b/solution.py
@@ -52,17 +52,17 @@
     return total
 
 
-def with_x_halo(buf, field, d=0):
-    own = buf[field, :, BASE + d : END + d, :]
+def halo_rows(buf, field, d=0):
     after = buf[field, :, END + d : END + d + SUB, :]
     before = buf[field, :, BASE - SUB + d : BASE + d, :]
-    halo = jnp.where(row_of(after.shape) < REACH, after, before)
-    return jnp.concatenate([own, halo], axis=1)
-
-
-def diff_x(buf, field, plus, wide):
-    if wide:
-        return weighted(lambda d: with_x_halo(buf, field, d), plus)
+    return jnp.where(row_of(after.shape) < REACH, after, before)
+
+
+def halo_diff_x(buf, field, plus):
+    return weighted(lambda d: halo_rows(buf, field, d), plus)
+
+
+def diff_x(buf, field, plus):
     return weighted(lambda d: buf[field, :, BASE + d : END + d, :], plus)
 
 
@@ -75,6 +75,22 @@
         return roll(jnp.where(lane < d if d > 0 else lane >= LANES + d, halo, field), -d)
 
     return weighted(shift, plus)
+
+
+def near_and_far(shift, plus):
+    sign = -1 if plus else 1
+    taps = [shift(sign * k) for k in range(REACH)]
+    near = far = None
+    for k in range(REACH):
+        one, two = coeffs[k] * taps[k], coeffs[REACH - 1 - k] * taps[k]
+        near = one if near is None else near + one
+        far = two if far is None else far + two
+    return near, far
+
+
+def ring_diff_y(field, plus):
+    near, far = near_and_far(lambda d: roll(field, -d), plus)
+    return roll(far, -REACH) - near if plus else near - roll(far, REACH)
 
 
 def diff_z(field, plus):
@@ -102,8 +118,7 @@
     return weighted(lambda d: buf[field, BASE + d : END + d, :], plus)
 
 
-def strip_y(field, plus):
-    return weighted(lambda d: roll(field, -d), plus)
+strip_y = ring_diff_y
 
 
 def strip_z(field, plus):
@@ -153,17 +168,61 @@
     return jnp.concatenate(tiles, axis=0)
 
 
-def y_halo_of_edges(low, high):
-    merged = jnp.where(lane_of(low.shape) % 16 < 8, low, high)
+def end_terms(lack, plus):
+    p = lane_of(lack.shape) % 16
+    before, after = jnp.where(p < 8, lack, 0.0), jnp.where(p < 8, 0.0, lack)
+    first_lanes = last_lanes = None
+    for k in range(1, REACH + 1):
+        first = k if plus else k - 1
+        second = first + 1 - 2 * k
+        if first > 0:
+            term = coeffs[k - 1] * roll(after, -first)
+            last_lanes = term if last_lanes is None else last_lanes + term
+        if second < 0:
+            term = coeffs[k - 1] * roll(before, -second)
+            first_lanes = -term if first_lanes is None else first_lanes - term
+    return jnp.where(p < 8, last_lanes, first_lanes)
+
+
+def at_ends(value):
+    lane = lane_of(value.shape)
+    return jnp.where((lane < REACH) | (lane >= LANES - REACH), value, 0.0)
+
+
+def ring_correction(edge, low, high, plus):
+    total = end_terms(jnp.where(lane_of(edge.shape) % 16 < 8, low, high) - edge, plus)
     return jnp.stack([
-        jnp.concatenate([roll(merged, 120 - 32 * z - 16 * tile) for tile in range(2)], axis=0)
+        jnp.concatenate([at_ends(roll(total, 120 - 32 * z - 16 * t)) for t in range(2)], axis=0)
         for z in range(LAYERS)
     ])
 
 
-def y_halo_of_strip(strip):
+def y_ends_of_strip(strip, plus):
     merged = jnp.where(lane_of(strip.shape) % 16 < 8, strip, roll(strip, -16))
-    return jnp.stack([roll(merged, 120 - 32 * z) for z in range(LAYERS)])
+    total = end_terms(merged, plus)
+    return jnp.stack([at_ends(roll(total, 120 - 32 * z)) for z in range(LAYERS)])
+
+
+def stencil_matrix(plus):
+    source = lax.broadcasted_iota(jnp.int32, (LANES, LANES), 0)
+    off = source - lane_of((LANES, LANES))
+    total = jnp.zeros((LANES, LANES), jnp.float32)
+    for k in range(1, REACH + 1):
+        first = k if plus else k - 1
+        total = jnp.where(off == first, coeffs[k - 1], total)
+        total = jnp.where(off == first + 1 - 2 * k, -coeffs[k - 1], total)
+    return total
+
+
+def inner_diff_y(fields, matrix):
+    rows = LAYERS * ROWS
+    stacked = jnp.concatenate([f.reshape(rows, LANES) for f in fields], axis=0)
+    out = jnp.dot(
+        stacked, matrix, precision=lax.Precision.HIGHEST, preferred_element_type=jnp.float32
+    )
+    return [
+        out[i * rows : (i + 1) * rows].reshape(LAYERS, ROWS, LANES) for i in range(len(fields))
+    ]
 
 
 def y_halo_of_corners(corner, g):
@@ -230,14 +289,28 @@
         self.side[...] = jnp.zeros_like(self.side)
         self.corners_in[...] = jnp.zeros_like(self.corners_in)
 
+    def pack(self, slot):
+        edges = []
+        for place in self.corner_places:
+            edges.append(pack_edge(self.own(slot, place)))
+            self.edge[slot, self.edges.index(place)] = edges[-1]
+        pack_corners(edges, self.corner, slot)
+
+    def pack_rest(self, slot):
+        for i, place in enumerate(self.edges):
+            if place not in self.corner_places:
+                self.edge[slot, i] = pack_edge(self.own(slot, place))
+
+    def start(self, slot, first, last):
+        for goes, _, copy in self.copies(slot)[first:last]:
+            pl.when(goes)(copy.start)
+
     def send(self, slot):
-        edges = {}
-        for i, place in enumerate(self.edges):
-            edges[place] = pack_edge(self.own(slot, place))
-            self.edge[slot, i] = edges[place]
-        pack_corners([edges[place] for place in self.corner_places], self.corner, slot)
-        for goes, _, copy in self.copies(slot):
-            pl.when(goes)(copy.start)
+        self.pack(slot)
+        self.start(slot, 0, 4)
+        self.start(slot, 6, 10)
+        self.pack_rest(slot)
+        self.start(slot, 4, 6)
 
     def wait_recv(self, slot):
         for _, arrives, copy in self.copies(slot):
@@ -257,9 +330,11 @@
         i = self.edges.index(place)
         return strip_of(self.edge[slot, i], self.side[slot, 0, i], self.side[slot, 1, i])
 
-    def y_halo(self, slot, place):
+    def ring_correction(self, slot, place, plus):
         i = self.edges.index(place)
-        return y_halo_of_edges(self.side[slot, 0, i], self.side[slot, 1, i])
+        return ring_correction(
+            self.edge[slot, i], self.side[slot, 0, i], self.side[slot, 1, i], plus
+        )
 
     def corner_tiles(self, slot):
         shape = (SUB, LANES)
@@ -271,10 +346,9 @@
                                  jnp.where(first, here[0], here[1])))
         return out
 
-    def wide_y_halo(self, slot, place, tiles):
+    def corner_y_halo(self, place, tiles):
         at = self.corner_places.index(place)
-        corner = y_halo_of_corners(tiles[at // 4], at % 4)
-        return jnp.concatenate([self.y_halo(slot, place), corner], axis=1)
+        return y_halo_of_corners(tiles[at // 4], at % 4)
 
     def set_strip_rows(self, place, strip, tiles):
         at = self.corner_places.index(place)
@@ -284,10 +358,9 @@
         self.strips[place, END : END + SUB, :] = rows
 
 
-def put_wide(work, place, value):
-    work[place, :, BASE:END, :] = value[:, :ROWS]
-    work[place, :, END : END + REACH, :] = value[:, ROWS : ROWS + REACH]
-    work[place, :, BASE - REACH : BASE, :] = value[:, ROWS + REACH :]
+def put_halo_rows(work, place, value):
+    work[place, :, END : END + REACH, :] = value[:, :REACH]
+    work[place, :, BASE - REACH : BASE, :] = value[:, REACH:]
 
 
 def log2(n):
@@ -329,7 +402,7 @@
     table_ref, src_ref, wav_ref, rec_ref, res_ref,
     f_buf, f_edge, f_side, f_corner, f_corners_in, f_strips,
     a_buf, a_edge, a_side, a_corner, a_corners_in, a_strips,
-    f_work, a_work, labels, lab, lab_edge, lab_side, mats, mats_s,
+    matrices, f_work, a_work, f_part, a_part, labels, lab, lab_edge, lab_side, mats, mats_s,
     inj_f, inj_s, inj_a, e_all, f_all, grads,
     in_sem, out_sem, f_send, f_recv, a_send, a_recv, l_send, l_recv,
 ):
@@ -390,9 +463,12 @@
 
     for copy in loads[1:first]:
         copy.wait()
+    for chain in (fwd, adj):
+        chain.pack(0)
+        chain.pack_rest(0)
     pl.semaphore_wait(barrier, len(around))
-    fwd.send(0)
-    adj.send(0)
+    fwd.start(0, 0, 10)
+    adj.start(0, 0, 10)
     for goes, _, copy in lab_copies:
         pl.when(goes)(copy.start)
 
@@ -421,6 +497,9 @@
         inj_a[t] = value.reshape(LAYERS, ROWS, LANES)
 
     spread(res_ref, row, at_y, LAYERS * ROWS, store_own)
+
+    matrices[0] = stencil_matrix(True)
+    matrices[1] = stencil_matrix(False)
 
     for _, arrives, copy in lab_copies:
         pl.when(arrives)(copy.wait_recv)
@@ -436,61 +515,79 @@
     shape = (LAYERS, wide, LANES)
     r = row_of(shape)
     inside = (r < ROWS) | ((r < ROWS + REACH) & (gx < nx - 1)) | ((r >= ROWS + REACH) & (gx > 0))
-    materials(with_x_halo(lab, 0), inside, mats)
+    both = jnp.concatenate([lab[0, :, BASE:END, :], halo_rows(lab, 0)], axis=1)
+    materials(both, inside, mats)
     lane = lane_of((ROWS, LANES))
     column = lane % 16 + jnp.where(lane % 32 < 16, -8, LANES - 8)
     inside = ((column >= 0) | (gy > 0)) & ((column < LANES) | (gy < ny - 1))
     materials(strip_of(lab_edge[0], lab_side[0, 0], lab_side[1, 0]), inside, mats_s)
 
+    own_mats = lambda prop: mats[prop, :, :ROWS]
+    halo_mats = lambda prop: mats[prop, :, ROWS:]
+    sxx, sxy, sxz, syy, syz, szz, vx, vy, vz = range(9)
+    f_terms = (
+        ((sxx, True), (sxy, False), (sxz, False)),
+        ((sxy, False), (syy, True), (syz, False)),
+        ((sxz, False), (syz, False), (szz, True)),
+    )
+
+    def forward_ahead(t):
+        slot = t % 2
+        for i, (_, (y, y_plus), (z, z_plus)) in enumerate(f_terms):
+            terms = ring_diff_y(fwd.own(slot, y), y_plus) + diff_z(fwd.own(slot, z), z_plus)
+            part = fwd.own(slot, vx + i) + own_mats(2) * terms
+            f_part[i] = part + inj_f[t, :, :ROWS] if i == 2 else part
+
     def forward_step(t):
-        slot = t % 2
-        other = 1 - slot
+        slot, other = t % 2, 1 - t % 2
         buf = f_buf.at[slot]
         fwd.wait_recv(slot)
         tiles = fwd.corner_tiles(slot)
-        div = []
-        sxx, sxy, sxz, syy, syz, szz, vx, vy, vz = range(9)
-        for first, second, third, plus in (
-            (sxx, sxy, sxz, 0), (sxy, syy, syz, 1), (sxz, syz, szz, 2)
-        ):
-            div.append(
-                diff_x(buf, first, plus == 0, True)
-                + diff_y(with_x_halo(buf, second), fwd.wide_y_halo(slot, second, tiles), plus == 1)
-                + diff_z(with_x_halo(buf, third), plus == 2)
-            )
-        strips = [fwd.strip(slot, place) for place in range(9)]
-        for place in (sxx, sxy, sxz):
-            fwd.set_strip_rows(place, strips[place], tiles)
-        strip_div = [
-            strip_x(f_strips, sxx, True) + strip_y(strips[sxy], False) + strip_z(strips[sxz], False),
-            strip_x(f_strips, sxy, False) + strip_y(strips[syy], True) + strip_z(strips[syz], False),
-            strip_x(f_strips, sxz, False) + strip_y(strips[syz], False) + strip_z(strips[szz], True),
-        ]
         if t > 0:
             fwd.wait_send(other)
-        halos = []
-        for i in range(3):
-            new = with_x_halo(buf, vx + i) + mats[2] * div[i]
-            side = strips[vx + i] + mats_s[2] * strip_div[i]
-            if i == 2:
-                new, side = new + inj_f[t], side + inj_s[t]
-            put_wide(f_work, i, new)
-            fwd.put(other, vx + i, new[:, :ROWS])
-            halos.append(y_halo_of_strip(side))
-        v = [fwd.own(other, vx + i) for i in range(3)]
+        strips = {}
+
+        def strip(place):
+            if place not in strips:
+                strips[place] = fwd.strip(slot, place)
+            return strips[place]
+
+        for place in (sxx, sxy, sxz):
+            fwd.set_strip_rows(place, strip(place), tiles)
+        v, ends = [], []
+        for i, ((x, x_plus), (y, y_plus), (z, z_plus)) in enumerate(f_terms):
+            terms = diff_x(buf, x, x_plus) + fwd.ring_correction(slot, y, y_plus)
+            v.append(f_part[i] + own_mats(2) * terms)
+            fwd.put(other, vx + i, v[i])
+            f_work[i, :, BASE:END, :] = v[i]
+            terms = (
+                halo_diff_x(buf, x, x_plus)
+                + diff_y(halo_rows(buf, y), fwd.corner_y_halo(y, tiles), y_plus)
+                + diff_z(halo_rows(buf, z), z_plus)
+            )
+            new = halo_rows(buf, vx + i) + halo_mats(2) * terms
+            put_halo_rows(f_work, i, new + inj_f[t, :, ROWS:] if i == 2 else new)
+            terms = (
+                strip_x(f_strips, x, x_plus)
+                + strip_y(strip(y), y_plus)
+                + strip_z(strip(z), z_plus)
+            )
+            side = strip(vx + i) + mats_s[2] * terms
+            ends.append(y_ends_of_strip(side + inj_s[t] if i == 2 else side, i != 1))
+        vx_y, vz_y = inner_diff_y((v[0], v[2]), matrices[0])
+        (vy_y,) = inner_diff_y((v[1],), matrices[1])
         strain = (
-            diff_x(f_work, 0, False, False),
-            diff_y(v[1], halos[1], False),
+            diff_x(f_work, 0, False),
+            vy_y + ends[1],
             diff_z(v[2], False),
-            diff_y(v[0], halos[0], True) + diff_x(f_work, 1, True, False),
-            diff_z(v[0], True) + diff_x(f_work, 2, True, False),
-            diff_z(v[1], True) + diff_y(v[2], halos[2], True),
+            vx_y + ends[0] + diff_x(f_work, 1, True),
+            diff_z(v[0], True) + diff_x(f_work, 2, True),
+            diff_z(v[1], True) + vz_y + ends[2],
         )
         for i in range(6):
             e_all[t, i] = strain[i]
-
         if t < steps - 1:
-            lam, shear = mats[0, :, :ROWS], mats[1, :, :ROWS]
+            lam, shear = own_mats(0), own_mats(1)
             exx, eyy, ezz, exy, exz, eyz = strain
             base, twice = lam * (exx + eyy + ezz), 2.0 * shear
             for place, inc in (
@@ -500,69 +597,87 @@
                 fwd.put(other, place, fwd.own(slot, place) + inc)
             fwd.send(other)
 
+    ux, uy, uz, qxx, qxy, qxz, qyy, qyz, qzz = range(9)
+
+    def adjoint_ahead(t):
+        u = [adj.own(t % 2, i) for i in range(3)]
+        a_part[0] = ring_diff_y(u[1], False)
+        a_part[1] = diff_z(u[2], False)
+        a_part[2] = ring_diff_y(u[0], True)
+        a_part[3] = diff_z(u[0], True)
+        a_part[4] = diff_z(u[1], True) + ring_diff_y(u[2], True)
+
     def adjoint_step(t):
-        slot = t % 2
-        other = 1 - slot
+        slot, other = t % 2, 1 - t % 2
         buf = a_buf.at[slot]
         adj.wait_recv(slot)
         tiles = adj.corner_tiles(slot)
-        vx, vy, vz, sxx, sxy, sxz, syy, syz, szz = range(9)
-        u = [with_x_halo(buf, i) for i in range(3)]
-        u_halo = [adj.wide_y_halo(slot, i, tiles) for i in range(2)]
-        u_own = adj.own(slot, vz)
-        exx, eyy, ezz = diff_x(buf, vx, False, True), diff_y(u[1], u_halo[1], False), diff_z(u[2], False)
-        exy = diff_y(u[0], u_halo[0], True) + diff_x(buf, vy, True, True)
-        exz = diff_z(u[0], True) + diff_x(buf, vz, True, True)
-        eyz = diff_z(adj.own(slot, vy), True) + diff_y(u_own, adj.y_halo(slot, vz), True)
-        for i, value in enumerate((exx, eyy, ezz, exy, exz)):
-            f_all[t, i] = value[:, :ROWS]
-        f_all[t, 5] = eyz
+        if t > 0:
+            adj.wait_send(other)
+
+        def put(place, value):
+            if t < steps - 1:
+                adj.put(other, place, value)
+            else:
+                out_ref[ADJ[place]] = value
+
         side = [adj.strip(slot, i) for i in range(3)]
         for i in range(2):
             adj.set_strip_rows(i, side[i], tiles)
-        side_xx, side_yy, side_zz = strip_x(a_strips, vx, False), strip_y(side[1], False), strip_z(side[2], False)
-        side_xy = strip_y(side[0], True) + strip_x(a_strips, vy, True)
-        side_yz = strip_z(side[1], True) + strip_y(side[2], True)
-        if t > 0:
-            adj.wait_send(other)
-        lam, shear = mats[0], mats[1]
-        base = lam * (exx + eyy + ezz)
+        xx, yy, zz = strip_x(a_strips, ux, False), strip_y(side[1], False), strip_z(side[2], False)
+        xy = strip_y(side[0], True) + strip_x(a_strips, uy, True)
+        yz = strip_z(side[1], True) + strip_y(side[2], True)
+        lam, shear = mats_s[0], mats_s[1]
+        ends = {}
+        for place, inc in (
+            (qxy, shear * xy), (qyy, lam * (xx + yy + zz) + 2.0 * shear * yy), (qyz, shear * yz)
+        ):
+            ends[place] = y_ends_of_strip(adj.strip(slot, place) - inc, place == qyy)
+        u = [halo_rows(buf, i) for i in range(3)]
+        u_halo = [adj.corner_y_halo(i, tiles) for i in range(2)]
+        exx, eyy = halo_diff_x(buf, ux, False), diff_y(u[1], u_halo[1], False)
+        exy = diff_y(u[0], u_halo[0], True) + halo_diff_x(buf, uy, True)
+        exz = diff_z(u[0], True) + halo_diff_x(buf, uz, True)
+        lam, shear = halo_mats(0), halo_mats(1)
+        base = lam * (exx + eyy + diff_z(u[2], False))
         for i, (place, inc) in enumerate(
-            ((sxx, base + 2.0 * shear * exx), (sxy, shear * exy), (sxz, shear * exz))
+            ((qxx, base + 2.0 * shear * exx), (qxy, shear * exy), (qxz, shear * exz))
         ):
-            new = with_x_halo(buf, place) - inc
-            put_wide(a_work, i, new)
-            adj.put(other, place, new[:, :ROWS])
-        base, shear = base[:, :ROWS], shear[:, :ROWS]
+            put_halo_rows(a_work, i, halo_rows(buf, place) - inc)
+        exx, ezz = diff_x(buf, ux, False), a_part[1]
+        eyy = a_part[0] + adj.ring_correction(slot, uy, False)
+        exy = a_part[2] + adj.ring_correction(slot, ux, True) + diff_x(buf, uy, True)
+        exz = a_part[3] + diff_x(buf, uz, True)
+        eyz = a_part[4] + adj.ring_correction(slot, uz, True)
+        for i, value in enumerate((exx, eyy, ezz, exy, exz, eyz)):
+            f_all[t, i] = value
+        lam, shear = own_mats(0), own_mats(1)
+        base, twice = lam * (exx + eyy + ezz), 2.0 * shear
+        q = {}
         for place, inc in (
-            (syy, base + 2.0 * shear * eyy[:, :ROWS]),
-            (syz, shear * eyz),
-            (szz, base + 2.0 * shear * ezz[:, :ROWS]),
+            (qxx, base + twice * exx), (qxy, shear * exy), (qxz, shear * exz),
+            (qyy, base + twice * eyy), (qyz, shear * eyz), (qzz, base + twice * ezz),
         ):
-            adj.put(other, place, adj.own(slot, place) - inc)
-        lam, shear = mats_s[0], mats_s[1]
-        side_inc = {
-            sxy: shear * side_xy,
-            syy: lam * (side_xx + side_yy + side_zz) + 2.0 * shear * side_yy,
-            syz: shear * side_yz,
-        }
-        halo = {
-            place: y_halo_of_strip(adj.strip(slot, place) - inc) for place, inc in side_inc.items()
-        }
-        new = {place: adj.own(other, place) for place in (sxy, sxz, syy, syz, szz)}
+            q[place] = adj.own(slot, place) - inc
+            put(place, q[place])
+        for i, place in enumerate((qxx, qxy, qxz)):
+            a_work[i, :, BASE:END, :] = q[place]
+        (qyy_y,) = inner_diff_y((q[qyy],), matrices[0])
+        qxy_y, qyz_y = inner_diff_y((q[qxy], q[qyz]), matrices[1])
         div = (
-            diff_x(a_work, 0, True, False) + diff_y(new[sxy], halo[sxy], False) + diff_z(new[sxz], False),
-            diff_x(a_work, 1, False, False) + diff_y(new[syy], halo[syy], True) + diff_z(new[syz], False),
-            diff_x(a_work, 2, False, False) + diff_y(new[syz], halo[syz], False) + diff_z(new[szz], True),
+            diff_x(a_work, 0, True) + qxy_y + ends[qxy] + diff_z(q[qxz], False),
+            diff_x(a_work, 1, False) + qyy_y + ends[qyy] + diff_z(q[qyz], False),
+            diff_x(a_work, 2, False) + qyz_y + ends[qyz] + diff_z(q[qzz], True),
         )
-        buoy = mats[2, :, :ROWS]
         for i in range(3):
-            value = adj.own(slot, i) - buoy * div[i]
-            adj.put(other, i, value + inj_a[t] if i == 2 else value)
+            value = adj.own(slot, i) - own_mats(2) * div[i]
+            put(i, value + inj_a[t] if i == 2 else value)
         if t < steps - 1:
             adj.send(other)
 
     for t in range(steps):
+        forward_ahead(t)
+        adjoint_ahead(t)
         forward_step(t)
         adjoint_step(t)
 
@@ -571,9 +686,6 @@
     adj.wait_send(last)
     for goes, _, copy in lab_copies:
         pl.when(goes)(copy.wait_send)
-
-    for place, number in enumerate(ADJ):
-        out_ref[number] = adj.own(1 - last, place)
 
     grad_l = grad_m = None
     for t in range(steps):
@@ -641,8 +753,11 @@
             pltpu.VMEM((1,) + rec.shape, jnp.int32),
             vmem(*res.shape),
         ] + chain(9, 2, 3) + chain(6, 1, 2) + [
+            vmem(2, LANES, LANES),
             vmem(3, LAYERS, PADDED, LANES),
             vmem(3, LAYERS, PADDED, LANES),
+            vmem(3, *block),
+            vmem(5, *block),
             pltpu.VMEM(block, jnp.int32),
             vmem(1, LAYERS, PADDED, LANES),
             vmem(1, *tile),

time: 34.4 us -> 32 us (0.930)
  Pallas kernels: 33.5 us -> 31.1 us
    pallas_call x1, Pallas kernels: 32.8 us -> 30.4 us  [shards(): pl.pallas_call(functools.partial(kernel, dims), out_shape=(pltpu.VMEM(fwd...]
where the time goes in v4:
time: 32 us; the launch traced here: 31.8 us
  Pallas kernels  31.1 us (97%)
  between operations  0.64 us (2%)
    pallas_call x1, Pallas kernels, shards(): pl.pallas_call(functools.partial(kernel, dims), out_shape=(pltpu.VMEM(fwd...  30.4 us
    pallas_call x1, Pallas kernels, shards(): pl.pallas_call(hand_over, out_shape=(pltpu.HBM(fwd.shape, f32), pltpu.HBM...  0.75 us

profile of v4, /device:TPU:24, one launch (start us, length us, event | category | flops | bytes accessed | tf_op | source)
XLA Modules:
  0.0 31.8 jit_solution(15267758067337313007)
XLA Ops:
  0.6 30.4 %shard_map.103 = (f32[9,4,16,128]{3,2,1,0:T(8,128)S(1)}, f32[4,16,128]{2,1,0:T(8,128)S(1)}, f32[4,16,128]{2,1,0:T(8,128)S(1)}) custom-call(f32[9,4,16,128]{3,2,1,0:T(8,128)} %fwd_hbm.1, f32[9,4,16,128]{3,2,1,0:T(8,128)} %adj_hbm.1, s32[4,16,128]{2,1,0:T(8,128)} %labels_hbm.1, f32[3,4]{1,0:T(4,128)} %table_hbm.1, s32[1,512]{1,0:T(1,128)} %bitcast.3, ...), custom_call_target="tpu_custom_call" | custom-call | tf_op jit(solution)/shard_map/pallas_call | solution.py:740
  31.0 0.8 %shard_map.104 = (f32[9,4,16,128]{3,2,1,0:T(8,128)}, f32[4,16,128]{2,1,0:T(8,128)}, f32[4,16,128]{2,1,0:T(8,128)}) custom-call(f32[9,4,16,128]{3,2,1,0:T(8,128)S(1)} %get-tuple-element.6.refs_0_, f32[4,16,128]{2,1,0:T(8,128)S(1)} %get-tuple-element.7.refs_1_, f32[4,16,128]{2,1,0:T(8,128)S(1)} %get-tuple-element.8.refs_2_), custom_call_target="tpu_custom_call" | custom-call | tf_op jit(solution)/shard_map/pallas_call | solution.py:781

commit v5 on v4

--- a/solution.py
+++ b/solution.py
@@ -21,13 +21,28 @@
 ADJ = (0, 1, 2, 3, 6, 7, 4, 8, 5)
 FWD_EDGES = tuple(range(9))
 ADJ_EDGES = (0, 1, 2, 4, 6, 7)
-FWD_CORNERS = (0, 1, 2, 3, 4)
+FWD_CORNERS = (1, 3, 4, 0, 2)
 ADJ_CORNERS = (0, 1)
 
 
 def place_in_grid():
     gx, gy = lax.axis_index("gx"), lax.axis_index("gy")
     return gx, gy, lax.axis_size("gx"), lax.axis_size("gy")
+
+
+def neighbours():
+    gx, gy, nx, ny = place_in_grid()
+    xs = {-1: lax.rem(gx + nx - 1, nx), 0: gx, 1: lax.rem(gx + 1, nx)}
+    ys = {-1: lax.rem(gy + ny - 1, ny), 0: gy, 1: lax.rem(gy + 1, ny)}
+    in_x, in_y = {-1: gx > 0, 1: gx < nx - 1}, {-1: gy > 0, 1: gy < ny - 1}
+    out = {}
+    for dx in (-1, 0, 1):
+        for dy in (-1, 0, 1):
+            if dx and dy:
+                out[dx, dy] = (xs[dx], ys[dy]), jnp.logical_and(in_x[dx], in_y[dy])
+            elif dx or dy:
+                out[dx, dy] = (xs[dx], ys[dy]), in_x[dx] if dx else in_y[dy]
+    return out
 
 
 def lane_of(shape):
@@ -64,17 +79,6 @@
 
 def diff_x(buf, field, plus):
     return weighted(lambda d: buf[field, :, BASE + d : END + d, :], plus)
-
-
-def diff_y(field, halo, plus):
-    lane = lane_of(field.shape)
-
-    def shift(d):
-        if d == 0:
-            return field
-        return roll(jnp.where(lane < d if d > 0 else lane >= LANES + d, halo, field), -d)
-
-    return weighted(shift, plus)
 
 
 def near_and_far(shift, plus):
@@ -215,18 +219,28 @@
 
 
 def inner_diff_y(fields, matrix):
-    rows = LAYERS * ROWS
+    shape = fields[0].shape
+    rows = shape[0] * shape[1]
     stacked = jnp.concatenate([f.reshape(rows, LANES) for f in fields], axis=0)
     out = jnp.dot(
         stacked, matrix, precision=lax.Precision.HIGHEST, preferred_element_type=jnp.float32
     )
-    return [
-        out[i * rows : (i + 1) * rows].reshape(LAYERS, ROWS, LANES) for i in range(len(fields))
-    ]
-
-
-def y_halo_of_corners(corner, g):
-    return jnp.stack([roll(corner, 124 - 32 * z - 8 * g) for z in range(LAYERS)])
+    return [out[i * rows : (i + 1) * rows].reshape(shape) for i in range(len(fields))]
+
+
+def corner_end_terms(corner):
+    first = lane_of(corner.shape) % 8 < 4
+    before, after = jnp.where(first, corner, 0.0), jnp.where(first, 0.0, corner)
+    back = [None] + [roll(before, k) for k in range(1, REACH + 1)]
+    ahead = [None] + [roll(after, -k) for k in range(1, REACH + 1)]
+
+    def total(terms, shift):
+        pairs = [(c, terms[k]) for k, c in enumerate(coeffs, shift) if k > 0]
+        return sum((c * term for c, term in pairs[1:]), pairs[0][0] * pairs[0][1])
+
+    p_stencil = jnp.where(first, total(ahead, 1), -total(back, 0))
+    m_stencil = jnp.where(first, total(ahead, 0), -total(back, 1))
+    return p_stencil, m_stencil
 
 
 def strip_rows_of_corners(corner, g):
@@ -235,34 +249,28 @@
 
 
 class Chain:
-    def __init__(self, refs, deep, shallow, edges, corners):
+    def __init__(self, refs, around, deep, shallow, edges, corners):
+        self.around = around
         (self.buf, self.edge, self.side, self.corner, self.corners_in,
          self.strips, self.send_sem, self.recv_sem) = refs
         self.deep, self.shallow = deep, shallow
         self.edges, self.corner_places = edges, corners
 
     def copies(self, slot):
-        gx, gy, nx, ny = place_in_grid()
         out = []
 
         def add(dx, dy, src, dst):
-            def inside(sx, sy):
-                conds = []
-                if sx:
-                    conds.append(gx > 0 if sx < 0 else gx < nx - 1)
-                if sy:
-                    conds.append(gy > 0 if sy < 0 else gy < ny - 1)
-                return conds[0] if len(conds) == 1 else jnp.logical_and(*conds)
-
+            to, goes = self.around[dx, dy]
+            _, arrives = self.around[-dx, -dy]
             copy = pltpu.make_async_remote_copy(
                 src_ref=src,
                 dst_ref=dst,
                 send_sem=self.send_sem.at[slot, len(out)],
                 recv_sem=self.recv_sem.at[slot, len(out)],
-                device_id=(lax.rem(gx + dx + nx, nx), lax.rem(gy + dy + ny, ny)),
+                device_id=to,
                 device_id_type=MESH,
             )
-            out.append((inside(dx, dy), inside(-dx, -dy), copy))
+            out.append((goes, arrives, copy))
 
         for dx in (-1, 1):
             for dy in (-1, 1):
@@ -346,9 +354,9 @@
                                  jnp.where(first, here[0], here[1])))
         return out
 
-    def corner_y_halo(self, place, tiles):
-        at = self.corner_places.index(place)
-        return y_halo_of_corners(tiles[at // 4], at % 4)
+    def corner_ends(self, place, totals):
+        g = self.corner_places.index(place)
+        return jnp.stack([at_ends(roll(totals, 124 - 32 * z - 8 * g)) for z in range(LAYERS)])
 
     def set_strip_rows(self, place, strip, tiles):
         at = self.corner_places.index(place)
@@ -410,10 +418,19 @@
     gx, gy, nx, ny = place_in_grid()
     steps = wav_ref.shape[0]
 
+    around = neighbours()
     fwd = Chain((f_buf, f_edge, f_side, f_corner, f_corners_in, f_strips, f_send, f_recv),
-                (0, 1, 2), (3, 4, 5, 6, 7, 8), FWD_EDGES, FWD_CORNERS)
+                around, (0, 1, 2), (3, 4, 5, 6, 7, 8), FWD_EDGES, FWD_CORNERS)
     adj = Chain((a_buf, a_edge, a_side, a_corner, a_corners_in, a_strips, a_send, a_recv),
-                (0, 1, 2), (3, 4, 5), ADJ_EDGES, ADJ_CORNERS)
+                around, (0, 1, 2), (3, 4, 5), ADJ_EDGES, ADJ_CORNERS)
+
+    fwd.clear()
+    adj.clear()
+    lab[...] = jnp.zeros_like(lab)
+    lab_side[...] = jnp.zeros_like(lab_side)
+    barrier = pltpu.get_barrier_semaphore()
+    for to, _ in around.values():
+        pl.semaphore_signal(barrier, inc=1, device_id=to, device_id_type=MESH)
 
     loads = []
 
@@ -424,10 +441,13 @@
 
     own_rows = pl.ds(BASE, ROWS)
     load(labels_hbm, labels)
-    for place, number in enumerate(FWD):
-        load(fwd_hbm.at[number], f_buf.at[0, place, :, own_rows, :])
-    for place, number in enumerate(ADJ):
-        load(adj_hbm.at[number], a_buf.at[0, place, :, own_rows, :])
+    for hbm, buf, order in ((fwd_hbm, f_buf, FWD), (adj_hbm, a_buf, ADJ)):
+        start = 0
+        for end in range(1, len(order) + 1):
+            if end == len(order) or order[end] != order[end - 1] + 1:
+                part = pl.ds(order[start], end - start)
+                load(hbm.at[part], buf.at[0, pl.ds(start, end - start), :, own_rows, :])
+                start = end
     first = len(loads)
     for src, dst in (
         (table_hbm, table_ref), (src_hbm, src_ref), (wav_hbm, wav_ref),
@@ -435,31 +455,23 @@
     ):
         load(src, dst)
 
-    fwd.clear()
-    adj.clear()
-    lab[...] = jnp.zeros_like(lab)
-    lab_side[...] = jnp.zeros_like(lab_side)
-    barrier = pltpu.get_barrier_semaphore()
-    around = [(dx, dy) for dx in (-1, 0, 1) for dy in (-1, 0, 1) if dx or dy]
-    for dx, dy in around:
-        to = (lax.rem(gx + dx + nx, nx), lax.rem(gy + dy + ny, ny))
-        pl.semaphore_signal(barrier, inc=1, device_id=to, device_id_type=MESH)
-
     loads[0].wait()
     lab[0, :, BASE:END, :] = labels[...].astype(jnp.float32)
     lab_edge[0] = pack_edge(lab[0, :, BASE:END, :])
     lab_copies = []
-    for goes, arrives, src, dst, axis, to in (
-        (gx > 0, gx < nx - 1, lab.at[0, :, pl.ds(BASE, REACH), :], lab.at[0, :, pl.ds(END, REACH), :], "gx", lax.rem(gx + nx - 1, nx)),
-        (gx < nx - 1, gx > 0, lab.at[0, :, pl.ds(END - REACH, REACH), :], lab.at[0, :, pl.ds(BASE - REACH, REACH), :], "gx", lax.rem(gx + 1, nx)),
-        (gy > 0, gy < ny - 1, lab_edge, lab_side.at[1], "gy", lax.rem(gy + ny - 1, ny)),
-        (gy < ny - 1, gy > 0, lab_edge, lab_side.at[0], "gy", lax.rem(gy + 1, ny)),
+    own_labels = lab.at[0]
+    for dx, dy, src, dst in (
+        (-1, 0, own_labels.at[:, pl.ds(BASE, REACH), :], own_labels.at[:, pl.ds(END, REACH), :]),
+        (1, 0, own_labels.at[:, pl.ds(END - REACH, REACH), :], own_labels.at[:, pl.ds(BASE - REACH, REACH), :]),
+        (0, -1, lab_edge, lab_side.at[1]),
+        (0, 1, lab_edge, lab_side.at[0]),
     ):
+        to, goes = around[dx, dy]
         copy = pltpu.make_async_remote_copy(
             src_ref=src, dst_ref=dst, send_sem=l_send.at[len(lab_copies)],
-            recv_sem=l_recv.at[len(lab_copies)], device_id={axis: to}, device_id_type=MESH,
+            recv_sem=l_recv.at[len(lab_copies)], device_id=to, device_id_type=MESH,
         )
-        lab_copies.append((goes, arrives, copy))
+        lab_copies.append((goes, around[-dx, -dy][1], copy))
 
     for copy in loads[1:first]:
         copy.wait()
@@ -533,6 +545,8 @@
 
     def forward_ahead(t):
         slot = t % 2
+        if t > 0:
+            fwd.wait_send(1 - slot)
         for i, (_, (y, y_plus), (z, z_plus)) in enumerate(f_terms):
             terms = ring_diff_y(fwd.own(slot, y), y_plus) + diff_z(fwd.own(slot, z), z_plus)
             part = fwd.own(slot, vx + i) + own_mats(2) * terms
@@ -543,8 +557,6 @@
         buf = f_buf.at[slot]
         fwd.wait_recv(slot)
         tiles = fwd.corner_tiles(slot)
-        if t > 0:
-            fwd.wait_send(other)
         strips = {}
 
         def strip(place):
@@ -554,6 +566,10 @@
 
         for place in (sxx, sxy, sxz):
             fwd.set_strip_rows(place, strip(place), tiles)
+        p_ends, m_ends = corner_end_terms(tiles[0])
+        halo_y = dict(zip((syy,), inner_diff_y((halo_rows(buf, syy),), matrices[0])))
+        halo_y.update(zip((sxy, syz), inner_diff_y(
+            (halo_rows(buf, sxy), halo_rows(buf, syz)), matrices[1])))
         v, ends = [], []
         for i, ((x, x_plus), (y, y_plus), (z, z_plus)) in enumerate(f_terms):
             terms = diff_x(buf, x, x_plus) + fwd.ring_correction(slot, y, y_plus)
@@ -562,7 +578,7 @@
             f_work[i, :, BASE:END, :] = v[i]
             terms = (
                 halo_diff_x(buf, x, x_plus)
-                + diff_y(halo_rows(buf, y), fwd.corner_y_halo(y, tiles), y_plus)
+                + halo_y[y] + fwd.corner_ends(y, p_ends if y_plus else m_ends)
                 + diff_z(halo_rows(buf, z), z_plus)
             )
             new = halo_rows(buf, vx + i) + halo_mats(2) * terms
@@ -600,6 +616,8 @@
     ux, uy, uz, qxx, qxy, qxz, qyy, qyz, qzz = range(9)
 
     def adjoint_ahead(t):
+        if t > 0:
+            adj.wait_send(1 - t % 2)
         u = [adj.own(t % 2, i) for i in range(3)]
         a_part[0] = ring_diff_y(u[1], False)
         a_part[1] = diff_z(u[2], False)
@@ -612,8 +630,6 @@
         buf = a_buf.at[slot]
         adj.wait_recv(slot)
         tiles = adj.corner_tiles(slot)
-        if t > 0:
-            adj.wait_send(other)
 
         def put(place, value):
             if t < steps - 1:
@@ -634,9 +650,10 @@
         ):
             ends[place] = y_ends_of_strip(adj.strip(slot, place) - inc, place == qyy)
         u = [halo_rows(buf, i) for i in range(3)]
-        u_halo = [adj.corner_y_halo(i, tiles) for i in range(2)]
-        exx, eyy = halo_diff_x(buf, ux, False), diff_y(u[1], u_halo[1], False)
-        exy = diff_y(u[0], u_halo[0], True) + halo_diff_x(buf, uy, True)
+        p_ends, m_ends = corner_end_terms(tiles[0])
+        (ux_y,), (uy_y,) = inner_diff_y((u[0],), matrices[0]), inner_diff_y((u[1],), matrices[1])
+        exx, eyy = halo_diff_x(buf, ux, False), uy_y + adj.corner_ends(uy, m_ends)
+        exy = ux_y + adj.corner_ends(ux, p_ends) + halo_diff_x(buf, uy, True)
         exz = diff_z(u[0], True) + halo_diff_x(buf, uz, True)
         lam, shear = halo_mats(0), halo_mats(1)
         base = lam * (exx + eyy + diff_z(u[2], False))

time: 32 us -> 31.6 us (0.988)
  no operation moved by 1% of the time
where the time goes in v5:
time: 31.6 us; the launch traced here: 31.5 us
  Pallas kernels  30.9 us (98%)
  between operations  0.64 us (2%)
    pallas_call x1, Pallas kernels, shards(): pl.pallas_call(functools.partial(kernel, dims), out_shape=(pltpu.VMEM(fwd...  30.2 us
    pallas_call x1, Pallas kernels, shards(): pl.pallas_call(hand_over, out_shape=(pltpu.HBM(fwd.shape, f32), pltpu.HBM...  0.75 us

profile of v5, /device:TPU:24, one launch (start us, length us, event | category | flops | bytes accessed | tf_op | source)
XLA Modules:
  0.0 31.5 jit_solution(8969621206541410964)
XLA Ops:
  0.6 30.2 %shard_map.103 = (f32[9,4,16,128]{3,2,1,0:T(8,128)S(1)}, f32[4,16,128]{2,1,0:T(8,128)S(1)}, f32[4,16,128]{2,1,0:T(8,128)S(1)}) custom-call(f32[9,4,16,128]{3,2,1,0:T(8,128)} %fwd_hbm.1, f32[9,4,16,128]{3,2,1,0:T(8,128)} %adj_hbm.1, s32[4,16,128]{2,1,0:T(8,128)} %labels_hbm.1, f32[3,4]{1,0:T(4,128)} %table_hbm.1, s32[1,512]{1,0:T(1,128)} %bitcast.3, ...), custom_call_target="tpu_custom_call" | custom-call | tf_op jit(solution)/shard_map/pallas_call | solution.py:757
  30.8 0.8 %shard_map.104 = (f32[9,4,16,128]{3,2,1,0:T(8,128)}, f32[4,16,128]{2,1,0:T(8,128)}, f32[4,16,128]{2,1,0:T(8,128)}) custom-call(f32[9,4,16,128]{3,2,1,0:T(8,128)S(1)} %get-tuple-element.6.refs_0_, f32[4,16,128]{2,1,0:T(8,128)S(1)} %get-tuple-element.7.refs_1_, f32[4,16,128]{2,1,0:T(8,128)S(1)} %get-tuple-element.8.refs_2_), custom_call_target="tpu_custom_call" | custom-call | tf_op jit(solution)/shard_map/pallas_call | solution.py:798

commit v6 on v5

--- a/solution.py
+++ b/solution.py
@@ -479,10 +479,12 @@
         chain.pack(0)
         chain.pack_rest(0)
     pl.semaphore_wait(barrier, len(around))
-    fwd.start(0, 0, 10)
-    adj.start(0, 0, 10)
+    fwd.start(0, 0, 6)
+    adj.start(0, 0, 6)
     for goes, _, copy in lab_copies:
         pl.when(goes)(copy.start)
+    fwd.start(0, 6, 10)
+    adj.start(0, 6, 10)
 
     for copy in loads[first:]:
         copy.wait()

time: 31.6 us -> 31.6 us (level)
  no operation moved by 1% of the time
where the time goes in v6:
time: 31.6 us; the launch traced here: 31.5 us
  Pallas kernels  30.9 us (98%)
  between operations  0.64 us (2%)
    pallas_call x1, Pallas kernels, shards(): pl.pallas_call(functools.partial(kernel, dims), out_shape=(pltpu.VMEM(fwd...  30.2 us
    pallas_call x1, Pallas kernels, shards(): pl.pallas_call(hand_over, out_shape=(pltpu.HBM(fwd.shape, f32), pltpu.HBM...  0.75 us

profile of v6, /device:TPU:24, one launch (start us, length us, event | category | flops | bytes accessed | tf_op | source)
XLA Modules:
  0.0 31.5 jit_solution(16235913889299394819)
XLA Ops:
  0.6 30.2 %shard_map.103 = (f32[9,4,16,128]{3,2,1,0:T(8,128)S(1)}, f32[4,16,128]{2,1,0:T(8,128)S(1)}, f32[4,16,128]{2,1,0:T(8,128)S(1)}) custom-call(f32[9,4,16,128]{3,2,1,0:T(8,128)} %fwd_hbm.1, f32[9,4,16,128]{3,2,1,0:T(8,128)} %adj_hbm.1, s32[4,16,128]{2,1,0:T(8,128)} %labels_hbm.1, f32[3,4]{1,0:T(4,128)} %table_hbm.1, s32[1,512]{1,0:T(1,128)} %bitcast.3, ...), custom_call_target="tpu_custom_call" | custom-call | tf_op jit(solution)/shard_map/pallas_call | solution.py:759
  30.8 0.8 %shard_map.104 = (f32[9,4,16,128]{3,2,1,0:T(8,128)}, f32[4,16,128]{2,1,0:T(8,128)}, f32[4,16,128]{2,1,0:T(8,128)}) custom-call(f32[9,4,16,128]{3,2,1,0:T(8,128)S(1)} %get-tuple-element.6.refs_0_, f32[4,16,128]{2,1,0:T(8,128)S(1)} %get-tuple-element.7.refs_1_, f32[4,16,128]{2,1,0:T(8,128)S(1)} %get-tuple-element.8.refs_2_), custom_call_target="tpu_custom_call" | custom-call | tf_op jit(solution)/shard_map/pallas_call | solution.py:800
